TPU v7x, 32 devices: a whole 2x2x4 slice. The times are simulated.
32 devices in a mesh: dp: 16 (over z, y, x), rep: 2 (over core).
Axes of the slice: x: 2, y: 2, z: 4, core: 2. Of those that a mesh axis runs over, the one named last changes fastest.
Arguments:
- mel: bfloat16 [64, 1024, 80], P('rep', 'dp'), may hold values from -6 to 6
- grad_post: bfloat16 [64, 1024, 80], P('rep', 'dp'), may hold values from -6 to 6
- lengths: int32 [64], replicated, may hold values from 256 to 1024, as said below
- regroup: int32 [2, 32], replicated, may hold values from 0 to 31, each once within a row
- w_first: bfloat16 [5, 512, 80], P(None, 'dp'), may hold values from -0.3125 to 0.3125
- w_mid: bfloat16 [3, 5, 512, 512], P(None, None, 'dp'), may hold values from -0.125 to 0.125
- w_last: bfloat16 [5, 512, 80], P(None, 'dp'), may hold values from -0.125 to 0.125
- gains: float32 [4, 512], replicated, may hold values from 0.1 to 1.9
- shifts: float32 [4, 512], replicated, may hold values from -3 to 3
- gain_last: float32 [80], replicated, may hold values from 0.1 to 1.9
- shift_last: float32 [80], replicated, may hold values from -3 to 3
Outputs:
- mel_post: bfloat16 [64, 1024, 80], P('rep', 'dp')
- grad_mel: bfloat16 [64, 1024, 80], P('rep', 'dp')
- grad_w_first: float32 [5, 512, 80], P(None, 'dp')
- grad_w_mid: float32 [3, 5, 512, 512], P(None, None, 'dp')
- grad_w_last: float32 [5, 512, 80], P(None, 'dp')
- grad_gains: float32 [4, 512], replicated
- grad_shifts: float32 [4, 512], replicated
- grad_gain_last: float32 [80], replicated
- grad_shift_last: float32 [80], replicated
Inputs may be any that keep to these rules, and one draw needn't show every extreme that they name: `lengths`: every replica group's 32 utterances include one of exactly 1024 frames.
All inputs are finite; a program needn't handle non-finite values.
Results may differ from a plain program's by a relative error of at most 0.015.
Values may be sent and summed in bfloat16 or wider, within the bound.
A program may use at most 192 MiB of HBM per device.

v0:
```python
import jax
import jax.numpy as jnp
from jax import lax
from jax.sharding import PartitionSpec as P

MB = 2


def shortened(value):

    def short(part):
        return part.astype(jnp.bfloat16) if part.dtype == jnp.float32 else part

    return jax.tree.map(short, value)


def shifted(hidden, offset):
    if offset == 0:
        return hidden
    frames = hidden.shape[1]
    reach = abs(offset)
    padded = jnp.pad(hidden, ((0, 0), (reach, reach), (0, 0)))
    return padded[:, reach + offset : reach + offset + frames]


def conv_forward(hidden, weight):
    centre = weight.shape[0] // 2
    running = jnp.einsum(
        "blc,cd->bld", shifted(hidden, -centre), weight[0], preferred_element_type=jnp.float32
    )
    for tap_index in range(1, weight.shape[0]):
        running = running + jnp.einsum(
            "blc,cd->bld",
            shifted(hidden, tap_index - centre),
            weight[tap_index],
            preferred_element_type=jnp.float32,
        )
    return running


def conv_backward(hidden, grad_values, weight):
    centre = weight.shape[0] // 2
    weight_grad = jnp.stack(
        [
            jnp.einsum(
                "blc,bld->cd",
                shifted(hidden, tap_index - centre),
                grad_values,
                preferred_element_type=jnp.float32,
            )
            for tap_index in range(weight.shape[0])
        ]
    )
    hidden_grad = jnp.einsum(
        "bld,cd->blc", shifted(grad_values, centre), weight[0], preferred_element_type=jnp.float32
    )
    for tap_index in range(1, weight.shape[0]):
        hidden_grad = hidden_grad + jnp.einsum(
            "bld,cd->blc",
            shifted(grad_values, centre - tap_index),
            weight[tap_index],
            preferred_element_type=jnp.float32,
        )
    return (weight_grad, hidden_grad)


def normalize(values, frame_mask, frame_count):
    first_sum, second_sum = lax.psum(
        (
            jnp.sum(values * frame_mask, axis=(0, 1)),
            jnp.sum(values * values * frame_mask, axis=(0, 1)),
        ),
        ("dp", "rep"),
    )
    centre = first_sum / frame_count
    spread = second_sum / frame_count - centre * centre
    scale_inv = lax.rsqrt(spread + 1e-05)
    return ((values - centre) * scale_inv, scale_inv)


def norm_backward(grad_out, normed, scale_inv, gain, frame_mask, frame_count):
    shift_grad, gain_grad = lax.psum(
        (jnp.sum(grad_out, axis=(0, 1)), jnp.sum(grad_out * normed, axis=(0, 1))), ("dp", "rep")
    )
    grad_values = (
        gain * scale_inv * (grad_out - shift_grad / frame_count - normed * gain_grad / frame_count)
    )
    return (frame_mask * grad_values, gain_grad, shift_grad)


def layer_list(fetched):
    middle = fetched[1].shape[0]
    return (
        [jnp.swapaxes(fetched[0], 1, 2)]
        + [fetched[1][layer] for layer in range(middle)]
        + [fetched[2]]
    )


def local(
    mel, grad_post, lengths, regroup, w_first, w_mid, w_last, gains, shifts, gain_last, shift_last
):
    devices_dp = lax.axis_size("dp")
    replicas = lax.axis_size("rep")
    dp_index = lax.axis_index("dp")
    rep_index = lax.axis_index("rep")
    group_size = regroup.shape[1]
    utt_dev = group_size // devices_dp
    utt_micro = utt_dev // MB
    frames_all = mel.shape[1] * devices_dp
    middle = w_mid.shape[0]
    offsets = (jnp.arange(replicas, dtype=jnp.int32) * group_size)[:, None]
    lens_order = lengths[(regroup + offsets).reshape(-1)].reshape(
        replicas, devices_dp, MB, utt_micro
    )
    counts = jnp.sum(lens_order, axis=(0, 1, 3)).astype(jnp.float32)
    own_lens = lax.dynamic_index_in_dim(
        lax.dynamic_index_in_dim(lens_order, rep_index, 0, False), dp_index, 0, False
    )
    frame_ids = jnp.arange(frames_all, dtype=jnp.int32)
    masks = (frame_ids[None, None, :] < own_lens[:, :, None]).astype(jnp.float32)[..., None]
    local_order = lax.dynamic_index_in_dim(regroup, rep_index, 0, False)
    moved_mel, moved_grad = (
        lax.all_to_all(mel[local_order], "dp", split_axis=0, concat_axis=1, tiled=True),
        lax.all_to_all(grad_post[local_order], "dp", split_axis=0, concat_axis=1, tiled=True),
    )
    gain_list = [gains[layer] for layer in range(middle + 1)] + [gain_last]
    shift_list = [shifts[layer] for layer in range(middle + 1)] + [shift_last]
    depth = middle + 2
    gain_grads = [jnp.zeros_like(entry) for entry in gain_list]
    shift_grads = [jnp.zeros_like(entry) for entry in shift_list]
    owned = (
        jnp.zeros(w_first.shape, jnp.float32),
        jnp.zeros(w_mid.shape, jnp.float32),
        jnp.zeros(w_last.shape, jnp.float32),
    )
    refined = []
    input_grads = []
    for micro_index in range(MB):
        mel_block = moved_mel[micro_index * utt_micro : (micro_index + 1) * utt_micro]
        grad_block = moved_grad[micro_index * utt_micro : (micro_index + 1) * utt_micro].astype(
            jnp.float32
        )
        frame_mask = masks[micro_index]
        frame_count = counts[micro_index]
        fetched = (
            lax.all_gather(w_first, "dp", axis=1, tiled=True),
            lax.all_gather(w_mid, "dp", axis=2, tiled=True),
            lax.all_gather(w_last, "dp", axis=1, tiled=True),
        )
        weights = layer_list(fetched)
        hidden = (mel_block.astype(jnp.float32) * frame_mask).astype(jnp.bfloat16)
        inputs = []
        kept = []
        for layer in range(depth):
            inputs.append(hidden)
            normed, scale_inv = normalize(
                conv_forward(hidden, weights[layer]), frame_mask, frame_count
            )
            kept.append((normed, scale_inv))
            activated = gain_list[layer] * normed + shift_list[layer]
            if layer < depth - 1:
                hidden = (frame_mask * jnp.tanh(activated)).astype(jnp.bfloat16)
            else:
                refined.append(
                    (mel_block.astype(jnp.float32) + frame_mask * activated).astype(jnp.bfloat16)
                )
        fetched = (
            lax.all_gather(w_first, "dp", axis=1, tiled=True),
            lax.all_gather(w_mid, "dp", axis=2, tiled=True),
            lax.all_gather(w_last, "dp", axis=1, tiled=True),
        )
        weights = layer_list(fetched)
        grad_out = frame_mask * grad_block
        weight_grads = [None] * depth
        for layer in reversed(range(depth)):
            normed, scale_inv = kept[layer]
            grad_values, gain_grad, shift_grad = norm_backward(
                grad_out, normed, scale_inv, gain_list[layer], frame_mask, frame_count
            )
            gain_grads[layer] = gain_grads[layer] + gain_grad
            shift_grads[layer] = shift_grads[layer] + shift_grad
            weight_grad, hidden_grad = conv_backward(
                inputs[layer], grad_values.astype(jnp.bfloat16), weights[layer]
            )
            weight_grads[layer] = weight_grad
            if layer > 0:
                before = kept[layer - 1]
                activated = jnp.tanh(gain_list[layer - 1] * before[0] + shift_list[layer - 1])
                grad_out = frame_mask * hidden_grad * (1.0 - activated * activated)
            else:
                input_grads.append((grad_block + frame_mask * hidden_grad).astype(jnp.bfloat16))
        local_grads = (
            jnp.swapaxes(weight_grads[0], 1, 2),
            jnp.stack(weight_grads[1 : depth - 1]),
            weight_grads[depth - 1],
        )
        pieces = (
            lax.psum_scatter(local_grads[0], "dp", scatter_dimension=1, tiled=True),
            lax.psum_scatter(local_grads[1], "dp", scatter_dimension=2, tiled=True),
            lax.psum_scatter(local_grads[2], "dp", scatter_dimension=1, tiled=True),
        )
        owned = tuple((total + piece for total, piece in zip(owned, pieces)))
    final_first, final_mid, final_last = jax.tree.map(
        lambda part: part.astype(jnp.float32), lax.psum(shortened(owned), "rep")
    )
    back_mel, back_grad = (
        lax.all_to_all(
            jnp.concatenate(refined, axis=0), "dp", split_axis=1, concat_axis=0, tiled=True
        ),
        lax.all_to_all(
            jnp.concatenate(input_grads, axis=0), "dp", split_axis=1, concat_axis=0, tiled=True
        ),
    )
    inverse = (
        jnp.zeros((group_size,), jnp.int32)
        .at[local_order]
        .set(jnp.arange(group_size, dtype=jnp.int32))
    )
    return (
        back_mel[inverse],
        back_grad[inverse],
        final_first,
        final_mid,
        final_last,
        jnp.stack(gain_grads[: depth - 1]),
        jnp.stack(shift_grads[: depth - 1]),
        gain_grads[depth - 1],
        shift_grads[depth - 1],
    )


def solution(mesh):
    in_specs = (
        P("rep", "dp", None),
        P("rep", "dp", None),
        P(),
        P(),
        P(None, "dp", None),
        P(None, None, "dp", None),
        P(None, "dp", None),
        P(),
        P(),
        P(),
        P(),
    )
    out_specs = (
        P("rep", "dp", None),
        P("rep", "dp", None),
        P(None, "dp", None),
        P(None, None, "dp", None),
        P(None, "dp", None),
        P(),
        P(),
        P(),
        P(),
    )
    return jax.shard_map(local, mesh=mesh, in_specs=in_specs, out_specs=out_specs, check_vma=False)
```

profile of v0, /device:TPU:0, one launch (start us, length us, event | category | flops | bytes accessed | tf_op | source)
XLA Modules:
  0.0 1261.3 jit_solution(4543719357968197157)
XLA Ops:
  10.1 8.4 all-to-all-start
  21.2 52.7 %all_gather.6 = bf16[5,512,80]{2,1,0:T(8,128)(2,1)S(1)} all-gather(bf16[5,32,80]{2,1,0:T(8,128)(2,1)S(1)} %copy-done.61), channel_id=1, replica_groups=mesh['dp'=16,'rep'=2] {'dp'}, dimensions={1}, use_global_device_ids=true | all-gather | bytes 435200 | tf_op jit(solution)/shard_map/all_gather | solution.py:147
  73.9 7.9 all-to-all-start.2
  81.9 50.4 %all_gather.8 = bf16[5,512,80]{2,1,0:T(8,128)(2,1)S(1)} all-gather(bf16[5,32,80]{2,1,0:T(8,128)(2,1)S(1)} %copy-done.62), channel_id=1, replica_groups=mesh['dp'=16,'rep'=2] {'dp'}, dimensions={1}, use_global_device_ids=true | all-gather | bytes 435200 | tf_op jit(solution)/shard_map/all_gather | solution.py:149
  137.3 2.4 copy.34
  139.6 2.3 slice_convert_fusion.1
  161.6 2.5 multiply_reduce_fusion.23
  164.1 2.5 multiply_reduce_fusion.15
  166.6 39.4 %all-reduce.49 = (f32[512]{0:T(512)S(1)}, f32[512]{0:T(512)S(1)}, f32[512]{0:T(512)S(1)}, f32[512]{0:T(512)S(1)}) all-reduce(f32[512]{0:T(512)S(1)} %get-tuple-element.43, f32[512]{0:T(512)S(1)} %get-tuple-element.42, f32[512]{0:T(512)S(1)} %get-tuple-element.51, ...), channel_id=1, replica_groups=mesh['dp'=16,'rep'=2] {'dp','rep'}, use_global_device_ids=true, to_apply=%region_4.5 | all-reduce | flops 2048 | bytes 16384 | tf_op jit(solution)/shard_map/psum | solution.py:68
  207.8 2.7 multiply_convert_fusion.15
  224.7 3.6 multiply_reduce_fusion.21
  228.2 3.5 multiply_reduce_fusion.13
  231.7 39.6 %all-reduce.48 = (f32[512]{0:T(512)S(1)}, f32[512]{0:T(512)S(1)}, f32[512]{0:T(512)S(1)}, f32[512]{0:T(512)S(1)}) all-reduce(f32[512]{0:T(512)S(1)} %get-tuple-element.41, f32[512]{0:T(512)S(1)} %get-tuple-element.40, f32[512]{0:T(512)S(1)} %get-tuple-element.49, ...), channel_id=1, replica_groups=mesh['dp'=16,'rep'=2] {'dp','rep'}, use_global_device_ids=true, to_apply=%region_8.9 | all-reduce | flops 2048 | bytes 16384 | tf_op jit(solution)/shard_map/psum | solution.py:68
  272.6 2.7 multiply_convert_fusion.14
  275.3 2.1 fusion.265
  289.8 3.5 multiply_reduce_fusion.19
  293.3 3.6 multiply_reduce_fusion.11
  296.9 41.0 %all-reduce.47 = (f32[512]{0:T(512)S(1)}, f32[512]{0:T(512)S(1)}, f32[512]{0:T(512)S(1)}, f32[512]{0:T(512)S(1)}) all-reduce(f32[512]{0:T(512)S(1)} %get-tuple-element.39, f32[512]{0:T(512)S(1)} %get-tuple-element.38, f32[512]{0:T(512)S(1)} %get-tuple-element.47, ...), channel_id=1, replica_groups=mesh['dp'=16,'rep'=2] {'dp','rep'}, use_global_device_ids=true, to_apply=%region_12.13 | all-reduce | flops 2048 | bytes 16384 | tf_op jit(solution)/shard_map/psum | solution.py:68
  339.1 2.7 multiply_convert_fusion.13
  341.9 2.1 fusion.269
  356.4 3.5 multiply_reduce_fusion.17
  359.9 3.6 multiply_reduce_fusion.9
  363.5 39.6 %all-reduce.46 = (f32[512]{0:T(512)S(1)}, f32[512]{0:T(512)S(1)}, f32[512]{0:T(512)S(1)}, f32[512]{0:T(512)S(1)}) all-reduce(f32[512]{0:T(512)S(1)} %get-tuple-element.37, f32[512]{0:T(512)S(1)} %get-tuple-element.36, f32[512]{0:T(512)S(1)} %get-tuple-element.45, ...), channel_id=1, replica_groups=mesh['dp'=16,'rep'=2] {'dp','rep'}, use_global_device_ids=true, to_apply=%region_16.17 | all-reduce | flops 2048 | bytes 16384 | tf_op jit(solution)/shard_map/psum | solution.py:68
  404.3 2.7 multiply_convert_fusion.12
  413.4 40.8 %all-reduce.45 = (f32[80]{0:T(128)S(1)}, f32[80]{0:T(128)S(1)}, f32[80]{0:T(128)S(1)}, f32[80]{0:T(128)S(1)}) all-reduce(f32[80]{0:T(128)S(1)} %get-tuple-element.69, f32[80]{0:T(128)S(1)} %get-tuple-element.68, f32[80]{0:T(128)S(1)} %get-tuple-element.71, f32[80]{0:T(128)S(1)} %get-tuple-element.70), channel_id=1, replica_groups=mesh['dp'=16,'rep'=2] {'dp','rep'}, use_global_device_ids=true, to_apply=%region_18.19 | all-reduce | flops 320 | bytes 2560 | tf_op jit(solution)/shard_map/psum | solution.py:68
  458.0 39.8 %all-reduce.44 = (f32[80]{0:T(128)S(1)}, f32[80]{0:T(128)S(1)}, f32[80]{0:T(128)S(1)}, f32[80]{0:T(128)S(1)}) all-reduce(f32[80]{0:T(128)S(1)} %multiply_reduce_fusion.26, f32[80]{0:T(128)S(1)} %get-tuple-element.156, f32[80]{0:T(128)S(1)} %multiply_reduce_fusion.24, ...), channel_id=1, replica_groups=mesh['dp'=16,'rep'=2] {'dp','rep'}, use_global_device_ids=true, to_apply=%region_45.46 | all-reduce | flops 320 | bytes 2560 | tf_op jit(solution)/shard_map/psum | solution.py:82
  499.5 2.5 multiply_convert_fusion.18
  509.0 3.2 fusion.467
  512.3 3.2 fusion.463
  515.4 41.0 %all-reduce.43 = (f32[512]{0:T(512)S(1)}, f32[512]{0:T(512)S(1)}, f32[512]{0:T(512)S(1)}, f32[512]{0:T(512)S(1)}) all-reduce(f32[512]{0:T(512)S(1)} %get-tuple-element.59, f32[512]{0:T(512)S(1)} %get-tuple-element.58, f32[512]{0:T(512)S(1)} %get-tuple-element.67, ...), channel_id=1, replica_groups=mesh['dp'=16,'rep'=2] {'dp','rep'}, use_global_device_ids=true, to_apply=%region_49.50 | all-reduce | flops 2048 | bytes 16384 | tf_op jit(solution)/shard_map/psum | solution.py:82
  557.7 3.6 multiply_convert_fusion.7
  565.1 2.7 copy-done.47
  577.7 2.8 fusion.466
  580.4 2.7 fusion.462
  583.2 39.4 %all-reduce.42 = (f32[512]{0:T(512)S(1)}, f32[512]{0:T(512)S(1)}, f32[512]{0:T(512)S(1)}, f32[512]{0:T(512)S(1)}) all-reduce(f32[512]{0:T(512)S(1)} %get-tuple-element.57, f32[512]{0:T(512)S(1)} %get-tuple-element.56, f32[512]{0:T(512)S(1)} %get-tuple-element.65, ...), channel_id=1, replica_groups=mesh['dp'=16,'rep'=2] {'dp','rep'}, use_global_device_ids=true, to_apply=%region_53.54 | all-reduce | flops 2048 | bytes 16384 | tf_op jit(solution)/shard_map/psum | solution.py:82
  623.8 3.6 multiply_convert_fusion.6
  631.2 2.7 copy-done.48
  643.8 2.8 fusion.465
  646.5 2.7 fusion.461
  649.3 41.3 %all-reduce.41 = (f32[512]{0:T(512)S(1)}, f32[512]{0:T(512)S(1)}, f32[512]{0:T(512)S(1)}, f32[512]{0:T(512)S(1)}) all-reduce(f32[512]{0:T(512)S(1)} %get-tuple-element.55, f32[512]{0:T(512)S(1)} %get-tuple-element.54, f32[512]{0:T(512)S(1)} %get-tuple-element.63, ...), channel_id=1, replica_groups=mesh['dp'=16,'rep'=2] {'dp','rep'}, use_global_device_ids=true, to_apply=%region_57.58 | all-reduce | flops 2048 | bytes 16384 | tf_op jit(solution)/shard_map/psum | solution.py:82
  691.8 3.5 multiply_convert_fusion.5
  713.6 2.7 copy-done.49
  717.3 9.5 maximum_add_fusion
  729.0 5.4 all-to-all-start.1
  749.1 4.0 fusion.464
  753.2 3.8 fusion.460
  757.0 48.9 %all-reduce.40 = (f32[512]{0:T(512)S(1)}, f32[512]{0:T(512)S(1)}, f32[512]{0:T(512)S(1)}, f32[512]{0:T(512)S(1)}) all-reduce(f32[512]{0:T(512)S(1)} %get-tuple-element.53, f32[512]{0:T(512)S(1)} %get-tuple-element.52, f32[512]{0:T(512)S(1)} %get-tuple-element.61, ...), channel_id=1, replica_groups=mesh['dp'=16,'rep'=2] {'dp','rep'}, use_global_device_ids=true, to_apply=%region_61.62 | all-reduce | flops 2048 | bytes 16384 | tf_op jit(solution)/shard_map/psum | solution.py:82
  807.1 5.4 multiply_convert_fusion
  817.3 3.1 copy.38
  820.4 2.4 fusion.47
  822.7 2.3 fusion.42
  825.0 2.3 fusion.46
  830.5 2.4 fusion.41
  832.9 2.2 fusion.40
  835.1 2.3 fusion.39
  838.5 2.5 add.890
  841.0 3.1 copy.39
  850.0 10.0 all-to-all-start.3
  860.0 205.0 %reduce-scatter.6.cloned.1.call-done = f32[3,5,32,512]{3,2,1,0:T(8,128)} async-done(((f32[3,5,512,512]{3,2,1,0:T(8,128)}), f32[3,5,32,512]{3,2,1,0:T(8,128)}) %reduce-scatter.6.cloned.1.call-update) | async-done | bytes 983056 | tf_op jit(solution)/shard_map/reduce_scatter | solution.py:200
  1073.3 80.4 %reduce-scatter.4.cloned.1.call-done = f32[5,32,80]{2,0,1:T(8,128)} async-done(((f32[5,512,80]{2,0,1:T(8,128)}), f32[5,32,80]{2,0,1:T(8,128)}) %reduce-scatter.4.cloned.1.call-update) | async-done | bytes 51216 | tf_op jit(solution)/shard_map/reduce_scatter | solution.py:199
  1154.7 79.1 %reduce-scatter.8.cloned.1.call-done = f32[5,32,80]{2,0,1:T(8,128)} async-done(((f32[5,512,80]{2,0,1:T(8,128)}), f32[5,32,80]{2,0,1:T(8,128)}) %reduce-scatter.8.cloned.1.call-update) | async-done | bytes 51216 | tf_op jit(solution)/shard_map/reduce_scatter | solution.py:201
  1234.7 3.8 all-reduce.50
  1239.8 12.7 %all-reduce.53.cloned.1.call-done = bf16[3,5,32,512]{3,2,1,0:T(8,128)(2,1)} async-done(((bf16[3,5,32,512]{3,2,1,0:T(8,128)(2,1)}), bf16[3,5,32,512]{3,2,1,0:T(8,128)(2,1)}) %all-reduce.53.cloned.1.call-update) | async-done | bytes 491536 | tf_op jit(solution)/shard_map/psum | solution.py:205
  1252.4 2.1 convert_element_type.551
  (411 shorter events, 187.1 us)
Async XLA Ops:
  7.2 12.8 %copy-start.79 = (s32[2,32]{1,0:T(2,128)S(1)}, s32[2,32]{1,0:T(2,128)}, u32[]{:S(2)}) copy-start(s32[2,32]{1,0:T(2,128)} %param.14) | copy-start | bytes 772
  7.2 11.4 copy-start.58
  7.2 13.0 %copy-start.2 = (s32[64]{0:T(128)S(1)}, s32[64]{0:T(128)}, u32[]{:S(2)}) copy-start(s32[64]{0:T(128)} %param.13) | copy-start | bytes 772
  7.2 13.9 %copy-start.61 = (bf16[5,32,80]{2,1,0:T(8,128)(2,1)S(1)}, bf16[5,32,80]{2,1,0:T(8,128)(2,1)}, u32[]{:S(2)}) copy-start(bf16[5,32,80]{2,1,0:T(8,128)(2,1)} %param.15) | copy-start | bytes 76804
  7.2 203.4 %all-gather.2.cloned.1.call-start = ((), (), s32[]{:S(2)}) async-start(), calls=%async_computation.7 | async-start | bytes 8355840 | tf_op jit(solution)/shard_map/all_gather | solution.py:148
  8.7 11.3 copy-start.84
  8.7 65.2 %copy-start.75 = (f32[4,512]{1,0:T(4,128)S(1)}, f32[4,512]{1,0:T(4,128)}, u32[]{:S(2)}) copy-start(f32[4,512]{1,0:T(4,128)} %param.19) | copy-start | bytes 24580
  10.1 71.8 %copy-start.62 = (bf16[5,32,80]{2,1,0:T(8,128)(2,1)S(1)}, bf16[5,32,80]{2,1,0:T(8,128)(2,1)}, u32[]{:S(2)}) copy-start(bf16[5,32,80]{2,1,0:T(8,128)(2,1)} %param.17) | copy-start | bytes 76804
  10.1 63.8 %all-to-all-start = ((bf16[32,64,80]{2,1,0:T(8,128)(2,1)}), bf16[32,64,80]{2,1,0:T(8,128)(2,1)S(1)}, u32[]{:S(2)}, u32[]{:S(2)}) async-start(bf16[32,64,80]{2,1,0:T(8,128)(2,1)} %gather_fusion), calls=%async_computation | async-start | bytes 1048576 | tf_op jit(solution)/shard_map/all_to_all | solution.py:124
  18.6 114.3 %copy-start.76 = (f32[4,512]{1,0:T(4,128)S(1)}, f32[4,512]{1,0:T(4,128)}, u32[]{:S(2)}) copy-start(f32[4,512]{1,0:T(4,128)} %param.18) | copy-start | bytes 24580
  73.8 90.3 %copy-start.34 = (bf16[5,512,80]{2,1,0:T(8,128)(2,1)}, bf16[5,512,80]{2,1,0:T(8,128)(2,1)S(1)}, u32[]{:S(2)}) copy-start(bf16[5,512,80]{2,1,0:T(8,128)(2,1)S(1)} %all_gather.6) | copy-start | bytes 1228804
  73.9 133.9 %copy-start.71 = (f32[1,512]{1,0:T(1,128)}, f32[1,512]{1,0:T(1,128)S(1)}, u32[]{:S(2)}) copy-start(f32[1,512]{1,0:T(1,128)S(1)} %get-tuple-element.146) | copy-start | bytes 6148
  73.9 63.4 %all-to-all-start.2 = ((bf16[32,64,80]{2,1,0:T(8,128)(2,1)}), bf16[32,64,80]{2,1,0:T(8,128)(2,1)}, u32[]{:S(2)}, u32[]{:S(2)}) async-start(bf16[32,64,80]{2,1,0:T(8,128)(2,1)} %gather_fusion.3), calls=%async_computation.2 | async-start | bytes 1048576 | tf_op jit(solution)/shard_map/all_to_all | solution.py:125
  81.8 983.2 %reduce-scatter.6.cloned.1.call-start = ((), (), s32[]{:S(2)}) async-start(), calls=%async_computation.10 | async-start | bytes 16711680 | tf_op jit(solution)/shard_map/reduce_scatter | solution.py:200
  132.9 74.9 %copy-start.59 = (f32[1,512]{1,0:T(1,128)}, f32[1,512]{1,0:T(1,128)S(1)}, u32[]{:S(2)}) copy-start(f32[1,512]{1,0:T(1,128)S(1)} %get-tuple-element.150) | copy-start | bytes 6148
  154.9 6.6 copy-start.38
  156.2 7.9 copy-start.36
  207.8 2.8 copy-start.67
  207.8 2.8 copy-start.69
  275.3 14.5 %copy-start.13 = (bf16[1024,512]{1,0:T(8,128)(2,1)}, bf16[1024,512]{1,0:T(8,128)(2,1)S(1)}, u32[]{:S(2)}) copy-start(bf16[1024,512]{1,0:T(8,128)(2,1)S(1)} %get-tuple-element.162) | copy-start | bytes 3145732
  275.3 18.0 %copy-start.7 = (bf16[1024,512]{1,0:T(8,128)(2,1)}, bf16[1024,512]{1,0:T(8,128)(2,1)S(1)}, u32[]{:S(2)}) copy-start(bf16[1024,512]{1,0:T(8,128)(2,1)S(1)} %get-tuple-element.163) | copy-start | bytes 3145732
  341.9 14.5 %copy-start.15 = (bf16[1024,512]{1,0:T(8,128)(2,1)}, bf16[1024,512]{1,0:T(8,128)(2,1)S(1)}, u32[]{:S(2)}) copy-start(bf16[1024,512]{1,0:T(8,128)(2,1)S(1)} %get-tuple-element.160) | copy-start | bytes 3145732
  341.9 18.0 %copy-start.10 = (bf16[1024,512]{1,0:T(8,128)(2,1)}, bf16[1024,512]{1,0:T(8,128)(2,1)S(1)}, u32[]{:S(2)}) copy-start(bf16[1024,512]{1,0:T(8,128)(2,1)S(1)} %get-tuple-element.161) | copy-start | bytes 3145732
  407.0 5.0 copy-start.5
  411.6 42.6 %copy-start.77 = (f32[80]{0:T(128)S(1)}, f32[80]{0:T(128)}, u32[]{:S(2)}) copy-start(f32[80]{0:T(128)} %param.20) | copy-start | bytes 964
  411.6 45.2 %copy-start.43 = (f32[1024,80]{0,1:T(8,128)S(1)}, f32[1024,80]{0,1:T(8,128)}, u32[]{:S(2)}) copy-start(f32[1024,80]{0,1:T(8,128)} %reshape.1645) | copy-start | bytes 983044
  411.6 87.8 %copy-start.78 = (f32[80]{0:T(128)S(1)}, f32[80]{0:T(128)}, u32[]{:S(2)}) copy-start(f32[80]{0:T(128)} %param.21) | copy-start | bytes 964
  497.7 5.5 copy-start.82
  497.7 7.0 copy-start.80
  509.0 3.2 copy-start.25
  557.7 3.6 copy-start.16
  563.5 4.2 copy-start.24
  563.5 4.2 copy-start.40
  564.3 6.5 slice-start
  567.7 3.1 slice-start.1
  569.1 7.7 copy-start.17
  623.8 3.6 copy-start.14
  629.6 4.2 copy-start.30
  629.7 4.2 copy-start.42
  630.4 6.5 slice-start.2
  633.9 3.1 slice-start.3
  635.2 7.7 copy-start.21
  695.3 3.0 copy-start.19
  711.3 4.9 slice-start.8
  711.3 4.9 slice-start.10
  712.0 4.3 slice-start.9
  712.0 5.3 slice-start.11
  729.0 121.0 %all-to-all-start.1 = ((bf16[2,1024,80]{2,0,1:T(2,128)(2,1)}), bf16[2,1024,80]{2,0,1:T(2,128)(2,1)}, u32[]{:S(2)}, u32[]{:S(2)}) async-start(bf16[2,1024,80]{2,0,1:T(2,128)(2,1)} %copy.31), calls=%async_computation.1 | async-start | bytes 1048576 | tf_op jit(solution)/shard_map/all_to_all | solution.py:208
  734.4 419.4 %reduce-scatter.4.cloned.1.call-start = ((), (), s32[]{:S(2)}) async-start(), calls=%async_computation.9 | async-start | bytes 2228224 | tf_op jit(solution)/shard_map/reduce_scatter | solution.py:199
  749.1 4.1 copy-start.32
  749.1 4.1 copy-start.64
  749.1 4.0 copy-start.66
  753.2 53.9 %copy-start.73 = (f32[512]{0:T(512)S(1)}, f32[512]{0:T(512)}, u32[]{:S(2)}) copy-start(f32[512]{0:T(512)} %get-tuple-element.114) | copy-start | bytes 6148
  753.2 53.9 %copy-start.74 = (f32[512]{0:T(512)S(1)}, f32[512]{0:T(512)}, u32[]{:S(2)}) copy-start(f32[512]{0:T(512)} %get-tuple-element.191) | copy-start | bytes 6148
  807.1 5.5 copy-start.39
  820.4 7.0 copy-start.6
  830.5 403.3 %reduce-scatter.8.cloned.1.call-start = ((), (), s32[]{:S(2)}) async-start(), calls=%async_computation.11 | async-start | bytes 2228224 | tf_op jit(solution)/shard_map/reduce_scatter | solution.py:201
  830.5 6.9 copy-start.4
  838.5 5.6 copy-start.35
  848.8 219.2 %copy-start.81 = (f32[80]{0:T(128)S(1)}, f32[80]{0:T(128)}, u32[]{:S(2)}) copy-start(f32[80]{0:T(128)} %copy-done.80) | copy-start | bytes 964
  848.8 219.2 %copy-start.83 = (f32[80]{0:T(128)S(1)}, f32[80]{0:T(128)}, u32[]{:S(2)}) copy-start(f32[80]{0:T(128)} %copy-done.82) | copy-start | bytes 964
  850.0 220.4 %all-to-all-start.3 = ((bf16[2,1024,80]{2,0,1:T(2,128)(2,1)}), bf16[2,1024,80]{2,0,1:T(2,128)(2,1)S(1)}, u32[]{:S(2)}, u32[]{:S(2)}) async-start(bf16[2,1024,80]{2,0,1:T(2,128)(2,1)} %copy.35), calls=%async_computation.3 | async-start | bytes 1048576 | tf_op jit(solution)/shard_map/all_to_all | solution.py:211
  860.0 392.4 %all-reduce.53.cloned.1.call-start = ((), (), s32[]{:S(2)}) async-start(), calls=%async_computation.8 | async-start | bytes 983040 | tf_op jit(solution)/shard_map/psum | solution.py:205
  1070.5 184.0 %copy-start.1 = (bf16[32,64,80]{2,1,0:T(8,128)(2,1)S(1)}, bf16[32,64,80]{2,1,0:T(8,128)(2,1)}, u32[]{:S(2)}) copy-start(bf16[32,64,80]{2,1,0:T(8,128)(2,1)} %param.11) | copy-start | bytes 983044
  (42 other events, 74.4 us)
Sparse Core Ops, SparseCore 0:
  10.8 137.8 all-gather.1
  727.0 338.0 reduce-scatter.5
  1067.3 86.3 reduce-scatter.3
  1155.9 77.8 reduce-scatter.7
  1236.6 15.7 all-reduce.52
where the time goes:
time: 1270 us; the launch traced here: 1260 us
  blocking collectives  518 us (41%)
  waiting for transfers between devices  378 us (30%)
  matrix products  188 us (15%)
  other arithmetic  77.8 us (6%)
  local copies, waits for them, and re-layouts  52.4 us (4%)
  starting transfers between devices  32 us (3%)
  between operations  15.7 us (1%)
    psum x5, blocking collectives, norm_backward(): lax.psum((jnp.sum(grad_out, axis=(0, 1)), jnp.sum(grad_out * normed, axis...  210 us
    reduce_scatter x1, waiting for transfers between devices, local(): lax.psum_scatter(local_grads[1], 'dp', scatter_dimension=2, tiled=True)  205 us
    psum x5, blocking collectives, normalize(): lax.psum((jnp.sum(values * frame_mask, axis=(0, 1)), jnp.sum(values * val...  200 us
    reduce_scatter x1, waiting for transfers between devices, local(): lax.psum_scatter(local_grads[0], 'dp', scatter_dimension=1, tiled=True)  80.4 us
    reduce_scatter x1, waiting for transfers between devices, local(): lax.psum_scatter(local_grads[2], 'dp', scatter_dimension=1, tiled=True)  79.1 us
    dot_general x40, matrix products, conv_forward(): jnp.einsum('blc,cd->bld', shifted(hidden, tap_index - centre), weight[tap...  67.8 us
    all_gather x1, blocking collectives, local(): lax.all_gather(w_first, 'dp', axis=1, tiled=True)  52.7 us
    dot_general x40, matrix products, conv_backward(): jnp.einsum('bld,cd->blc', shifted(grad_values, centre - tap_index), weigh...  52.5 us
  transfers between devices with their start and end apart: 9, of which 4 were waited for; matrix products, arithmetic and copies ran while one was open for 10% of the time, Pallas kernels for 0%

commit v1 on v0

--- a/solution.py
+++ b/solution.py
@@ -1,9 +1,687 @@
+import functools
+
 import jax
 import jax.numpy as jnp
 from jax import lax
+from jax.experimental import pallas as pl
+from jax.experimental.pallas import tpu as pltpu
 from jax.sharding import PartitionSpec as P
 
 MB = 2
+PLANE = 4
+CORES = 2
+SUB = 16
+LANES = 128
+MESH = pl.DeviceIdType.MESH
+bf16 = jnp.bfloat16
+f32 = jnp.float32
+EPS = 1e-05
+
+
+def nn(a, b):
+    return jnp.dot(a, b, preferred_element_type=f32)
+
+
+def nt(a, b):
+    return lax.dot_general(a, b, (((1,), (1,)), ((), ())), preferred_element_type=f32)
+
+
+def tn(a, b):
+    return lax.dot_general(a, b, (((0,), (0,)), ((), ())), preferred_element_type=f32)
+
+
+def kernel(
+    n_dp, utts, frames, chans, mels, taps, middle,
+    len_s, reg_s, mel, gpost, wf, wm, wl, gains, shifts, gl, sl,
+    o_mel, o_grad, o_wf, o_wm, o_wl, o_gains, o_shifts, o_gl, o_sl,
+    mel_s, grd_s, bak_s, bak2_s, mel_r, grd_r, bak_r, bak2_r,
+    mel_p, grd_p, mask, h0, h, xh, xl, z, zl, gz, gzl,
+    W, WF, WL, rbufs,
+    ar_s, ar_r, ar_t, a1, a2, invs, glp, slp, lens,
+    ars_sem, arr_sem, a2a_s, a2a_r, gz_s, gz_r, gp_s, gp_r, gq_s, gq_r, gb_s, gb_r,
+    r0_s, r0_r, r1_s, r1_r, r2_s, r2_r, r3_s, r3_r, ro_s, ro_r,
+):
+    nz = n_dp // PLANE
+    total = n_dp * CORES
+    T = n_dp * frames
+    HALO = 2 * SUB
+    MT = T // 2
+    CL = chans // LANES
+    ctile = 32
+    dp = lax.axis_index("dp")
+    rep = lax.axis_index("rep")
+    zc = lax.div(dp, PLANE)
+    s = lax.rem(dp, PLANE)
+    sx = s + 1 - 2 * lax.rem(s, 2)
+    sy = s + 2 - 4 * lax.div(s, 2)
+    s1 = sx + rep * (sy - sx)
+    s2 = sy + rep * (sx - sy)
+    sd = 3 - s
+    lin = dp * CORES + rep
+    other = 1 - rep
+    sib = (dp, other)
+    peer1 = (zc * PLANE + s1, rep)
+    peer2 = (zc * PLANE + s2, rep)
+
+    def send(src, dst, ss, rs, to):
+        pltpu.make_async_remote_copy(
+            src_ref=src, dst_ref=dst, send_sem=ss, recv_sem=rs, device_id=to, device_id_type=MESH
+        ).start()
+
+    def wait(ref, sem):
+        pltpu.make_async_copy(ref, ref, sem).wait()
+
+    W[:, :, zc, s] = wm[...]
+    WF[:, zc, s] = jnp.zeros((taps, CORES) + WF.shape[4:], bf16)
+    WL[:, zc, s] = jnp.zeros((taps, CORES) + WL.shape[4:], bf16)
+    WF[:, zc, s, :, :, 0:mels] = wf[...]
+    WL[:, zc, s, :, :, 0:mels] = wl[...]
+
+    barrier = pltpu.get_barrier_semaphore()
+    for i in range(1, total):
+        to = lax.rem(lin + i, total)
+        pl.semaphore_signal(
+            barrier, inc=1, device_id=(lax.div(to, CORES), lax.rem(to, CORES)), device_id_type=MESH
+        )
+
+    mel_s[...] = jnp.zeros(mel_s.shape, bf16)
+    grd_s[...] = jnp.zeros(grd_s.shape, bf16)
+
+    @pl.loop(0, utts)
+    def _(k):
+        u = reg_s[rep, k]
+        mel_s[k, :, 0:mels] = mel[u]
+        grd_s[k, :, 0:mels] = gpost[u]
+
+    pl.semaphore_wait(barrier, total - 1)
+
+    def chunk(c):
+        if c == 0:
+            return WF
+        if c == middle + 1:
+            return WL
+        return W.at[c - 1]
+
+    def g0(c):
+        w = chunk(c)
+        for i in range(1, nz):
+            to = lax.rem(zc + i, nz) * PLANE + s
+            piece = w.at[:, zc, s, rep]
+            send(piece, piece, gz_s.at[c], gz_r.at[c], (to, rep))
+
+    def three(w):
+        return w.at[:, pl.ds(0, nz - 1), 0, 0]
+
+    def g1(c):
+        w = chunk(c)
+        wait(three(w), gz_r.at[c])
+        col = w.at[:, :, s, rep]
+        send(col, col, gp_s.at[c], gp_r.at[c], peer1)
+        send(col, col, gq_s.at[c], gq_r.at[c], peer2)
+        send(col, col, gb_s.at[c], gb_r.at[c], sib)
+
+    def g2(c):
+        w = chunk(c)
+        wait(w.at[:, :, 0, 0], gp_r.at[c])
+        col = w.at[:, :, s1, rep]
+        send(col, col, gq_s.at[c], gq_r.at[c], peer2)
+        send(col, col, gb_s.at[c], gb_r.at[c], sib)
+
+    def g3(c):
+        w = chunk(c)
+        wait(w.at[:, :, pl.ds(0, 2), 0], gq_r.at[c])
+        for q in (s2, sd):
+            col = w.at[:, :, q, rep]
+            send(col, col, gb_s.at[c], gb_r.at[c], sib)
+
+    def g4(c):
+        wait(chunk(c).at[:, :, :, 0], gb_r.at[c])
+
+    def gdrain(c):
+        w = chunk(c)
+        wait(three(w), gz_s.at[c])
+        wait(w.at[:, :, 0, 0], gp_s.at[c])
+        wait(w.at[:, :, pl.ds(0, 2), 0], gq_s.at[c])
+        wait(w.at[:, :, :, 0], gb_s.at[c])
+
+    def deal(src, dst, which):
+        for i in range(1, n_dp):
+            to = lax.rem(dp + i, n_dp)
+            send(
+                src.at[pl.ds(to * MB, MB)], dst.at[dp], a2a_s.at[which], a2a_r.at[which], (to, rep)
+            )
+        dst[dp] = src[pl.ds(dp * MB, MB)]
+
+    def dealt(dst, which):
+        wait(dst.at[pl.ds(0, n_dp - 1)], a2a_r.at[which])
+
+    def back(src, dst, which):
+        for i in range(1, n_dp):
+            to = lax.rem(dp + i, n_dp)
+            send(
+                src.at[to], dst.at[pl.ds(dp * MB, MB)], a2a_s.at[which], a2a_r.at[which], (to, rep)
+            )
+        dst[pl.ds(dp * MB, MB)] = src[dp]
+
+    def backed(dst, which):
+        wait(dst.at[pl.ds(0, utts - MB)], a2a_r.at[which])
+
+    def ar_go(rd, v1, v2):
+        n = v1.shape[1] // LANES
+        for i in range(CL):
+            for base, v in ((0, v1), (CL, v2)):
+                if i < n:
+                    row = v[:, i * LANES : (i + 1) * LANES]
+                else:
+                    row = jnp.zeros((1, LANES), f32)
+                ar_s[rd, base + i : base + i + 1, :] = row
+                ar_r[rd, lin, base + i : base + i + 1, :] = row
+        for i in range(1, total):
+            to = lax.rem(lin + i, total)
+            send(
+                ar_s.at[rd], ar_r.at[rd, lin], ars_sem.at[rd], arr_sem.at[rd],
+                (lax.div(to, CORES), lax.rem(to, CORES)),
+            )
+
+    def ar_get(rd, n):
+        wait(ar_r.at[rd, pl.ds(0, total - 1)], arr_sem.at[rd])
+        acc = ar_r[rd, 0]
+        for i in range(1, total):
+            acc = acc + ar_r[rd, i]
+        ar_t[...] = acc
+        v1 = jnp.concatenate([ar_t[i : i + 1, :] for i in range(n)], axis=1)
+        v2 = jnp.concatenate([ar_t[CL + i : CL + i + 1, :] for i in range(n)], axis=1)
+        return v1, v2
+
+    def fold(v):
+        return jnp.sum(v.reshape(v.shape[0] // 8, 8, v.shape[1]), axis=0)
+
+    def wide(mk, d):
+        return jnp.concatenate([mk] * (d // LANES), axis=1) if d > LANES else mk
+
+    def clear(d):
+        a1[:, 0:d] = jnp.zeros((8, d), f32)
+        a2[:, 0:d] = jnp.zeros((8, d), f32)
+
+    def ar_acc(rd, d):
+        ar_go(
+            rd,
+            jnp.sum(a1[:, 0:d], axis=0, keepdims=True),
+            jnp.sum(a2[:, 0:d], axis=0, keepdims=True),
+        )
+
+    def halo(ref):
+        d = ref.shape[1]
+        row = lax.rem(lax.broadcasted_iota(jnp.int32, (HALO, d), 0), SUB)
+        low = pltpu.roll(ref[T : T + HALO, :].astype(f32), 1, 0)
+        ref[0:HALO, :] = jnp.where(row == 0, 0.0, low).astype(bf16)
+        high = pltpu.roll(ref[HALO : 2 * HALO, :].astype(f32), HALO - 1, 0)
+        ref[T + HALO : T + 2 * HALO, :] = jnp.where(row == SUB - 1, 0.0, high).astype(bf16)
+
+    cnt = []
+    own = []
+    for m in range(MB):
+
+        def body(j, c, m=m):
+            for r in range(CORES):
+                c = c + len_s[r * utts + reg_s[r, j * MB + m]]
+            return c
+
+        cnt.append(lax.fori_loop(0, n_dp, body, jnp.int32(0)).astype(f32))
+        own.append(len_s[rep * utts + reg_s[rep, dp * MB + m]])
+
+    last = middle + 1
+
+    def mean_inv(rd, m, n):
+        v1, v2 = ar_get(rd, n)
+        mean = v1 / cnt[m]
+        var = v2 / cnt[m] - mean * mean
+        inv = lax.rsqrt(var + EPS)
+        invs[rd, 0:1, 0 : n * LANES] = inv
+        return mean, inv
+
+    def conv(layer, m):
+        rd = layer * MB + m
+        d = LANES if layer == last else chans
+        dst = zl if layer == last else z
+        clear(d)
+
+        @pl.loop(0, T // MT)
+        def _(t):
+            base = pl.multiple_of(t * MT, MT)
+            acc = None
+            for k in range(taps):
+                rows = pl.ds(base + SUB * k, MT)
+                if layer == 0:
+                    part = nt(h0[m, rows, :], WF[k].reshape(chans, LANES))
+                elif layer == last:
+                    part = nn(h[layer - 1, m, rows, :], WL[k].reshape(chans, LANES))
+                else:
+                    part = nn(h[layer - 1, m, rows, :], W[layer - 1, k].reshape(chans, chans))
+                acc = part if acc is None else acc + part
+            dst[m, pl.ds(base, MT), :] = acc
+            zm = acc * wide(mask[m, pl.ds(base, MT), :], d)
+            a1[:, 0:d] += fold(zm)
+            a2[:, 0:d] += fold(zm * acc)
+
+        ar_acc(rd, d)
+
+    def norm(layer, m):
+        mean, inv = mean_inv(layer * MB + m, m, CL)
+        g = gains[layer : layer + 1, :]
+        b = shifts[layer : layer + 1, :]
+
+        @pl.loop(0, T // ctile)
+        def _(i):
+            base = pl.multiple_of(i * ctile, ctile)
+            rows = pl.ds(base, ctile)
+            xv = (z[m, rows, :] - mean) * inv
+            hv = wide(mask[m, rows, :], chans) * jnp.tanh(g * xv + b)
+            xh[layer, m, rows, :] = xv.astype(bf16)
+            h[layer, m, pl.ds(base + HALO, ctile), :] = hv.astype(bf16)
+
+        halo(h.at[layer, m])
+
+    def grad_tail(layer, m, base, acc):
+        g = gains[layer : layer + 1, :]
+        b = shifts[layer : layer + 1, :]
+        rows = pl.ds(base, MT)
+        xv = xh[layer, m, rows, :].astype(f32)
+        th = jnp.tanh(g * xv + b)
+        gy = wide(mask[m, rows, :], chans) * acc * (1.0 - th * th)
+        z[m, rows, :] = gy
+        a1[...] += fold(gy)
+        a2[...] += fold(gy * xv)
+
+    def bround(layer, m):
+        return (last + 1 + layer) * MB + m
+
+    def coefs(layer, m, n, g, og, os):
+        v1, v2 = ar_get(bround(layer, m), n)
+        if m == 0:
+            og(v2, False)
+            os(v1, False)
+        else:
+            og(v2, True)
+            os(v1, True)
+        a = g * invs[layer * MB + m, 0:1, 0 : n * LANES]
+        return a, a * v1 / cnt[m], a * v2 / cnt[m]
+
+    def grad_z(layer, m):
+        def og(v, add):
+            o_gains[layer : layer + 1, :] = v + o_gains[layer : layer + 1, :] if add else v
+
+        def os(v, add):
+            o_shifts[layer : layer + 1, :] = v + o_shifts[layer : layer + 1, :] if add else v
+
+        a, c1, c2 = coefs(layer, m, CL, gains[layer : layer + 1, :], og, os)
+
+        @pl.loop(0, T // ctile)
+        def _(i):
+            base = pl.multiple_of(i * ctile, ctile)
+            rows = pl.ds(base, ctile)
+            v = a * z[m, rows, :] - c1 - c2 * xh[layer, m, rows, :].astype(f32)
+            gz[m, pl.ds(base + HALO, ctile), :] = (wide(mask[m, rows, :], chans) * v).astype(bf16)
+
+        halo(gz.at[m])
+
+    def grad_h(layer, m):
+        clear(chans)
+
+        @pl.loop(0, T // MT)
+        def _(t):
+            base = pl.multiple_of(t * MT, MT)
+            acc = None
+            for k in range(taps):
+                rows = pl.ds(base + SUB * (taps - 1 - k), MT)
+                if layer == last:
+                    part = nt(gzl[m, rows, :], WL[k].reshape(chans, LANES))
+                else:
+                    part = nt(gz[m, rows, :], W[layer - 1, k].reshape(chans, chans))
+                acc = part if acc is None else acc + part
+            grad_tail(layer - 1, m, base, acc)
+
+        ar_acc(bround(layer - 1, m), chans)
+
+    def wgrad(layer):
+        gdrain(layer)
+        w = chunk(layer)
+
+        @pl.loop(0, taps)
+        def _(k):
+            if layer == 0:
+                rows = pl.ds(pl.multiple_of(SUB * k, SUB), T)
+                acc = tn(gz[0, HALO : HALO + T, :], h0[0, rows, :])
+                for m in range(1, MB):
+                    acc = acc + tn(gz[m, HALO : HALO + T, :], h0[m, rows, :])
+            else:
+                g = gzl if layer == last else gz
+                rows = pl.ds(pl.multiple_of(SUB * (taps - 1 - k), SUB), T)
+                acc = tn(h[layer - 1, 0, HALO : HALO + T, :], g[0, rows, :])
+                for m in range(1, MB):
+                    acc = acc + tn(h[layer - 1, m, HALO : HALO + T, :], g[m, rows, :])
+            w[k] = acc.astype(bf16).reshape(w.shape[1:])
+
+        send(w.at[:, :, :, other], rbuf(layer)[0], r0_s.at[layer], r0_r.at[layer], sib)
+
+    def rbuf(layer):
+        return rbufs[layer]
+
+    def total_of(a, b):
+        return (a.astype(f32) + b.astype(f32)).astype(bf16)
+
+    def ra(layer):
+        w = chunk(layer)
+        r0, r1 = rbuf(layer)[0:2]
+        wait(r0, r0_r.at[layer])
+        for k in range(taps):
+            r0[k] = total_of(r0[k], w[k, :, :, rep])
+        for slot, q in ((1, sd), (0, s2)):
+            send(r0.at[:, :, q], r1.at[slot], r1_s.at[layer], r1_r.at[layer], peer2)
+
+    def rb(layer):
+        r0, r1, r2 = rbuf(layer)[0:3]
+        wait(r1, r1_r.at[layer])
+        for slot, q in ((1, s1), (0, s)):
+            for k in range(taps):
+                r1[slot, k] = total_of(r1[slot, k], r0[k, :, q])
+        send(r1.at[1], r2, r2_s.at[layer], r2_r.at[layer], peer1)
+
+    def rc(layer):
+        r1, r2, r3 = rbuf(layer)[1:4]
+        wait(r2, r2_r.at[layer])
+        for k in range(taps):
+            r2[k] = total_of(r2[k], r1[0, k])
+        for i in range(1, nz):
+            zt = lax.rem(zc + i, nz)
+            send(
+                r2.at[:, zt], r3.at[i - 1], r3_s.at[layer], r3_r.at[layer],
+                (zt * PLANE + s, rep),
+            )
+
+    def outs(layer):
+        return o_wf if layer == 0 else o_wl if layer == last else o_wm.at[layer - 1]
+
+    def rd_(layer):
+        r2, r3 = rbuf(layer)[2:4]
+        fs, fr = rbuf(layer)[4:6]
+        wait(r3, r3_r.at[layer])
+        out = outs(layer)
+        for k in range(taps):
+            v = r2[k, zc].astype(f32)
+            for i in range(nz - 1):
+                v = v + r3[i, k].astype(f32)
+            fs[k] = v
+            out[k, rep] = v[:, 0 : out.shape[3]]
+        send(fs, fr, ro_s.at[layer], ro_r.at[layer], sib)
+
+    def rdrain(layer):
+        r0, r1, r2, r3, fs, fr = rbuf(layer)
+        out = outs(layer)
+        wait(fr, ro_r.at[layer])
+        for k in range(taps):
+            out[k, other] = fr[k][:, 0 : out.shape[3]]
+        wait(fs, ro_s.at[layer])
+        wait(r0, r0_s.at[layer])
+        wait(r1, r1_s.at[layer])
+        wait(r2, r2_s.at[layer])
+        wait(r3, r3_s.at[layer])
+
+    g0(0)
+    deal(mel_s, mel_r, 0)
+    for c in range(1, last + 1):
+        g0(c)
+    glp[...] = jnp.zeros(glp.shape, f32)
+    slp[...] = jnp.zeros(slp.shape, f32)
+    glp[0:1, 0:mels] = gl[...]
+    slp[0:1, 0:mels] = sl[...]
+    for m in range(MB):
+
+        @pl.loop(0, T // ctile)
+        def _(i):
+            base = pl.multiple_of(i * ctile, ctile)
+            r = base + lax.broadcasted_iota(jnp.int32, (ctile, LANES), 0)
+            t = lax.rem(r, SUB) * frames + lax.div(r, SUB)
+            mask[m, pl.ds(base, ctile), :] = jnp.where(t < own[m], 1.0, 0.0)
+
+    g1(0)
+    g1(1)
+    g2(0)
+    g2(1)
+    g3(0)
+    dealt(mel_r, 0)
+    for m in range(MB):
+        for j in range(n_dp):
+            mel_p.at[m][pl.ds(j, frames, stride=SUB), :] = mel_r[j, m].astype(f32)
+        h0[m, HALO : HALO + T, :] = (mel_p[m] * mask[m]).astype(bf16)
+        halo(h0.at[m])
+    g1(2)
+    g4(0)
+    conv(0, 0)
+    g3(1)
+    conv(0, 1)
+    g2(2)
+    g4(1)
+    for layer in range(1, last + 1):
+        for m in range(MB):
+            norm(layer - 1, m)
+            conv(layer, m)
+            if m == 0:
+                if layer + 2 <= last:
+                    g1(layer + 2)
+            else:
+                if layer == 1:
+                    deal(grd_s, grd_r, 1)
+                if layer + 1 <= last:
+                    g3(layer + 1)
+                    if layer + 2 <= last:
+                        g2(layer + 2)
+                    g4(layer + 1)
+
+    dealt(grd_r, 1)
+    g_last = glp[0:1, :]
+    b_last = slp[0:1, :]
+    for m in range(MB):
+        for j in range(n_dp):
+            grd_p.at[m][pl.ds(j, frames, stride=SUB), :] = grd_r[j, m].astype(f32)
+        mean, inv = mean_inv(last * MB + m, m, 1)
+        clear(LANES)
+        ct = 64
+
+        @pl.loop(0, T // ct)
+        def _(i):
+            rows = pl.ds(pl.multiple_of(i * ct, ct), ct)
+            mk = mask[m, rows, :]
+            xv = (zl[m, rows, :] - mean) * inv
+            xl[m, rows, :] = xv
+            mel_p[m, rows, :] = mel_p[m, rows, :] + mk * (g_last * xv + b_last)
+            gy = mk * grd_p[m, rows, :]
+            a1[:, 0:LANES] += fold(gy)
+            a2[:, 0:LANES] += fold(gy * xv)
+
+        ar_acc(bround(last, m), LANES)
+    for m in range(MB):
+        for j in range(n_dp):
+            bak_s[j, m] = mel_p.at[m][pl.ds(j, frames, stride=SUB), :].astype(bf16)
+    back(bak_s, bak_r, 2)
+    for m in range(MB):
+
+        def og(v, add):
+            v = v[:, 0:mels]
+            o_gl[...] = o_gl[...] + v if add else v
+
+        def os(v, add):
+            v = v[:, 0:mels]
+            o_sl[...] = o_sl[...] + v if add else v
+
+        a, c1, c2 = coefs(last, m, 1, g_last, og, os)
+        ct = 64
+
+        @pl.loop(0, T // ct)
+        def _(i):
+            base = pl.multiple_of(i * ct, ct)
+            rows = pl.ds(base, ct)
+            v = a * grd_p[m, rows, :] - c1 - c2 * xl[m, rows, :]
+            gzl[m, pl.ds(base + HALO, ct), :] = (mask[m, rows, :] * v).astype(bf16)
+
+        halo(gzl.at[m])
+        grad_h(last, m)
+    wgrad(last)
+    for layer in range(middle, 0, -1):
+        for m in range(MB):
+            grad_z(layer, m)
+            grad_h(layer, m)
+            if m == 0:
+                ra(layer + 1)
+                if layer + 2 <= last:
+                    rc(layer + 2)
+            else:
+                rb(layer + 1)
+                if layer + 2 <= last:
+                    rd_(layer + 2)
+        wgrad(layer)
+    for m in range(MB):
+        grad_z(0, m)
+
+        @pl.loop(0, T // MT)
+        def _(t):
+            base = pl.multiple_of(t * MT, MT)
+            acc = None
+            for k in range(taps):
+                rows = pl.ds(base + SUB * (taps - 1 - k), MT)
+                part = nn(gz[m, rows, :], WF[k].reshape(chans, LANES))
+                acc = part if acc is None else acc + part
+            rows = pl.ds(base, MT)
+            grd_p[m, rows, :] = grd_p[m, rows, :] + mask[m, rows, :] * acc
+
+        if m == 0:
+            ra(1)
+            rc(2)
+        for j in range(n_dp):
+            bak2_s[j, m] = grd_p.at[m][pl.ds(j, frames, stride=SUB), :].astype(bf16)
+    back(bak2_s, bak2_r, 3)
+    wgrad(0)
+    rb(1)
+    ra(0)
+    rd_(2)
+
+    @pl.loop(0, utts)
+    def _(u):
+        def body(k, c):
+            return jnp.where(reg_s[rep, k] == u, k, c)
+
+        lens[u] = lax.fori_loop(0, utts, body, jnp.int32(0))
+
+    backed(bak_r, 2)
+
+    @pl.loop(0, utts)
+    def _(u):
+        o_mel[u] = bak_r[lens[u], :, 0:mels]
+
+    rc(1)
+    rb(0)
+    rd_(1)
+    rc(0)
+    backed(bak2_r, 3)
+
+    @pl.loop(0, utts)
+    def _(u):
+        o_grad[u] = bak2_r[lens[u], :, 0:mels]
+
+    rd_(0)
+    for layer in range(last + 1):
+        rdrain(layer)
+    wait(mel_r.at[pl.ds(0, n_dp - 1)], a2a_s.at[0])
+    wait(grd_r.at[pl.ds(0, n_dp - 1)], a2a_s.at[1])
+    wait(bak_r.at[pl.ds(0, utts - MB)], a2a_s.at[2])
+    wait(bak2_r.at[pl.ds(0, utts - MB)], a2a_s.at[3])
+
+    @pl.loop(0, 2 * (last + 1) * MB)
+    def _(r):
+        wait(ar_r.at[r, pl.ds(0, total - 1)], ars_sem.at[r])
+
+
+def local_kernel(
+    mel, grad_post, lengths, regroup, w_first, w_mid, w_last, gains, shifts, gain_last, shift_last
+):
+    n_dp = lax.axis_size("dp")
+    nz = n_dp // PLANE
+    utts, frames, mels = mel.shape
+    middle, taps, shard, chans = w_mid.shape
+    depth = middle + 2
+    T = n_dp * frames
+    TH = T + 4 * SUB
+    rows = shard // CORES
+    total = n_dp * CORES
+    rounds = 2 * depth * MB
+    V = pltpu.VMEM
+    D = pltpu.SemaphoreType.DMA
+    S = jax.ShapeDtypeStruct
+    out_shape = (
+        S(mel.shape, bf16),
+        S(mel.shape, bf16),
+        S((taps, CORES, rows, mels), f32),
+        S((middle, taps, CORES, rows, chans), f32),
+        S((taps, CORES, rows, mels), f32),
+        S(gains.shape, f32),
+        S(gains.shape, f32),
+        S((1, mels), f32),
+        S((1, mels), f32),
+    )
+    frame_buf = V((utts, frames, LANES), bf16)
+    frame_buf2 = V((n_dp, MB, frames, LANES), bf16)
+    landing = [
+        [
+            V((taps, nz, PLANE, rows, d), bf16),
+            V((2, taps, nz, rows, d), bf16),
+            V((taps, nz, rows, d), bf16),
+            V((nz - 1, taps, rows, d), bf16),
+            V((taps, rows, d), f32),
+            V((taps, rows, d), f32),
+        ]
+        for d in [LANES] + [chans] * middle + [LANES]
+    ]
+    scratch = [
+        frame_buf, frame_buf, frame_buf2, frame_buf2, frame_buf2, frame_buf2, frame_buf, frame_buf,
+        V((MB, T, LANES), f32), V((MB, T, LANES), f32), V((MB, T, LANES), f32),
+        V((MB, TH, LANES), bf16), V((middle + 1, MB, TH, chans), bf16),
+        V((middle + 1, MB, T, chans), bf16), V((MB, T, LANES), f32),
+        V((MB, T, chans), f32), V((MB, T, LANES), f32),
+        V((MB, TH, chans), bf16), V((MB, TH, LANES), bf16),
+        V((middle, taps, nz, PLANE, CORES, rows, chans), bf16),
+        V((taps, nz, PLANE, CORES, rows, LANES), bf16),
+        V((taps, nz, PLANE, CORES, rows, LANES), bf16),
+        landing,
+        V((rounds, 8, LANES), f32), V((rounds, total, 8, LANES), f32), V((8, LANES), f32),
+        V((8, chans), f32), V((8, chans), f32), V((depth * MB, 8, chans), f32),
+        V((8, LANES), f32), V((8, LANES), f32), pltpu.SMEM((utts,), jnp.int32),
+        D((rounds,)), D((rounds,)), D((4,)), D((4,)),
+    ] + [D((depth,))] * 18
+    body = functools.partial(kernel, n_dp, utts, frames, chans, mels, taps, middle)
+    vmem = pl.BlockSpec(memory_space=pltpu.VMEM)
+    smem = pl.BlockSpec(memory_space=pltpu.SMEM)
+    out = pl.pallas_call(
+        body,
+        out_shape=out_shape,
+        in_specs=[smem, smem] + [vmem] * 9,
+        out_specs=(vmem,) * 9,
+        scratch_shapes=scratch,
+        compiler_params=pltpu.CompilerParams(
+            collective_id=0, has_side_effects=True, vmem_limit_bytes=64 * 2**20
+        ),
+        name="postnet_step",
+    )(
+        lengths, regroup, mel, grad_post,
+        w_first.reshape(taps, CORES, rows, mels),
+        w_mid.reshape(middle, taps, CORES, rows, chans),
+        w_last.reshape(taps, CORES, rows, mels),
+        gains, shifts, gain_last[None, :], shift_last[None, :],
+    )
+    return (
+        out[0], out[1],
+        out[2].reshape(w_first.shape), out[3].reshape(w_mid.shape), out[4].reshape(w_last.shape),
+        out[5], out[6], out[7][0], out[8][0],
+    )
 
 
 def shortened(value):
@@ -255,4 +933,5 @@
         P(),
         P(),
     )
-    return jax.shard_map(local, mesh=mesh, in_specs=in_specs, out_specs=out_specs, check_vma=False)
+    step = local_kernel if mesh.shape["dp"] == SUB and mesh.shape["rep"] == CORES else local
+    return jax.shard_map(step, mesh=mesh, in_specs=in_specs, out_specs=out_specs, check_vma=False)

time: 1270 us -> 253 us (0.20)
  blocking collectives: 518 us -> 0 us
  waiting for transfers between devices: 378 us -> 0 us
  Pallas kernels: 0 us -> 245 us
  matrix products: 188 us -> 0 us
  other arithmetic: 77.8 us -> 0 us
  local copies, waits for them, and re-layouts: 52.4 us -> 7.7 us
  starting transfers between devices: 32 us -> 0 us
  between operations: 15.7 us -> 0.68 us
    psum x11 -> x0, blocking collectives: 415 us -> none  [the longest x5 210 us: norm_backward(): lax.psum((jnp.sum(grad_out, axis=(0, 1)), jnp.sum(grad_out * normed, axis...]
    reduce_scatter x3 -> x0, waiting for transfers between devices: 365 us -> none  [the longest x1 205 us: local(): lax.psum_scatter(local_grads[1], 'dp', scatter_dimension=2, tiled=True)]
    pallas_call x0 -> x1, Pallas kernels: none -> 245 us  [local_kernel(): pl.pallas_call(body, out_shape=out_shape, in_specs=[smem, smem] + [vmem]...]
    dot_general x150 -> x0, matrix products: 188 us -> none  [the longest x40 67.8 us: conv_forward(): jnp.einsum('blc,cd->bld', shifted(hidden, tap_index - centre), weight[tap...]
    all_gather x2 -> x0, blocking collectives: 103 us -> none  [the longest x1 52.7 us: local(): lax.all_gather(w_first, 'dp', axis=1, tiled=True)]
    convert_element_type x21 -> x0, other arithmetic: 44.3 us -> none  [the longest x9 23.9 us: local(): grad_values.astype(jnp.bfloat16)]
    all_to_all x4 -> x0, starting transfers between devices: 31.8 us -> none  [the longest x1 10 us: local(): lax.all_to_all(jnp.concatenate(input_grads, axis=0), 'dp', split_axis=1,...]
    add x14 -> x0, other arithmetic: 20.3 us -> none  [the longest x3 13.1 us: local(): owned = tuple((total + piece for total, piece in zip(owned, pieces)))]
  transfers between devices with their start and end apart: 9 -> 0, of which waited for: 4 -> 0; matrix products, arithmetic and copies ran while one was open for 10% -> 0% of each run, Pallas kernels for 0% -> 0%
where the time goes in v1:
time: 253 us
  Pallas kernels  245 us (97%)
  local copies, waits for them, and re-layouts  7.7 us (3%)
    pallas_call x1, Pallas kernels, local_kernel(): pl.pallas_call(body, out_shape=out_shape, in_specs=[smem, smem] + [vmem]...  245 us
    unnamed x25, local copies, waits for them, and re-layouts  7.7 us

profile of v1, /device:TPU:0, one launch (start us, length us, event | category | flops | bytes accessed | tf_op | source)
XLA Modules:
  0.0 253.0 jit_solution(114959232083067171)
XLA Ops:
  0.6 244.7 %postnet_step.1 = (bf16[32,64,80]{2,1,0:T(8,128)(2,1)}, bf16[32,64,80]{2,1,0:T(8,128)(2,1)}, f32[5,2,16,80]{3,2,1,0:T(8,128)}, f32[3,5,2,16,512]{4,3,2,1,0:T(8,1...) custom-call(s32[64]{0:T(128)} %len_s.1, ...), custom_call_target="tpu_custom_call" | custom-call | tf_op jit(solution)/shard_map/postnet_step/pallas_call | solution.py:663
  245.3 0.0 copy-start.1
  245.3 0.0 copy-start
  245.3 2.0 copy.29
  247.3 0.0 copy-done.1
  247.3 0.0 copy-start.3
  247.3 0.8 copy.30
  248.1 0.1 copy-done.3
  248.3 0.6 copy.31
  248.9 0.0 copy-done
  248.9 0.0 copy-start.2
  248.9 0.9 copy.32
  249.8 0.0 copy-done.2
  249.8 0.0 copy-start.5
  249.9 0.6 copy.33
  250.5 0.1 copy-done.5
  250.5 0.0 copy-start.4
  250.5 0.6 copy.34
  251.1 0.1 copy-done.4
  251.2 0.0 copy-start.7
  251.3 0.6 copy.35
  251.8 0.0 copy-done.7
  251.9 0.0 copy-start.6
  251.9 0.5 copy.36
  252.4 0.2 copy-done.6
  252.5 0.5 copy.37
Async XLA Ops:
  245.3 2.0 copy-start.1
  245.3 3.6 %copy-start = (f32[3,5,2,16,512]{4,3,2,1,0:T(8,128)S(1)}, f32[3,5,2,16,512]{4,3,2,1,0:T(8,128)}, u32[]{:S(2)}) copy-start(f32[3,5,2,16,512]{4,3,2,1,0:T(8,128)} %get-tuple-element.21) | copy-start | bytes 2949124
  247.3 0.9 copy-start.3
  248.9 0.9 copy-start.2
  249.8 0.7 copy-start.5
  250.5 0.7 copy-start.4
  251.2 0.6 copy-start.7
  251.9 0.7 copy-start.6

commit v2 on v1

--- a/solution.py
+++ b/solution.py
@@ -35,9 +35,9 @@
     len_s, reg_s, mel, gpost, wf, wm, wl, gains, shifts, gl, sl,
     o_mel, o_grad, o_wf, o_wm, o_wl, o_gains, o_shifts, o_gl, o_sl,
     mel_s, grd_s, bak_s, bak2_s, mel_r, grd_r, bak_r, bak2_r,
-    mel_p, grd_p, mask, h0, h, xh, xl, z, zl, gz, gzl,
-    W, WF, WL, rbufs,
-    ar_s, ar_r, ar_t, a1, a2, invs, glp, slp, lens,
+    mel_p, grd_p, mask, h0, h, xh, z, zl, gz, gzl,
+    W, WF, WL, GF, G1, rbufs,
+    ar_s, ar_r, ar_t, a1, a2, a3, a4, invs, glp, slp, lens,
     ars_sem, arr_sem, a2a_s, a2a_r, gz_s, gz_r, gp_s, gp_r, gq_s, gq_r, gb_s, gb_r,
     r0_s, r0_r, r1_s, r1_r, r2_s, r2_r, r3_s, r3_r, ro_s, ro_r,
 ):
@@ -166,16 +166,17 @@
     def backed(dst, which):
         wait(dst.at[pl.ds(0, utts - MB)], a2a_r.at[which])
 
-    def ar_go(rd, v1, v2):
-        n = v1.shape[1] // LANES
-        for i in range(CL):
-            for base, v in ((0, v1), (CL, v2)):
-                if i < n:
+    def ar_go(rd, vs):
+        n = 8 // len(vs)
+        for q, v in enumerate(vs):
+            for i in range(n):
+                if (i + 1) * LANES <= v.shape[1]:
                     row = v[:, i * LANES : (i + 1) * LANES]
                 else:
                     row = jnp.zeros((1, LANES), f32)
-                ar_s[rd, base + i : base + i + 1, :] = row
-                ar_r[rd, lin, base + i : base + i + 1, :] = row
+                at = q * n + i
+                ar_s[rd, at : at + 1, :] = row
+                ar_r[rd, lin, at : at + 1, :] = row
         for i in range(1, total):
             to = lax.rem(lin + i, total)
             send(
@@ -189,9 +190,11 @@
         for i in range(1, total):
             acc = acc + ar_r[rd, i]
         ar_t[...] = acc
-        v1 = jnp.concatenate([ar_t[i : i + 1, :] for i in range(n)], axis=1)
-        v2 = jnp.concatenate([ar_t[CL + i : CL + i + 1, :] for i in range(n)], axis=1)
-        return v1, v2
+        q = CL if n == CL else 2
+        return [
+            jnp.concatenate([ar_t[e * q + i : e * q + i + 1, :] for i in range(n)], axis=1)
+            for e in range(8 // q)
+        ]
 
     def fold(v):
         return jnp.sum(v.reshape(v.shape[0] // 8, 8, v.shape[1]), axis=0)
@@ -202,13 +205,13 @@
     def clear(d):
         a1[:, 0:d] = jnp.zeros((8, d), f32)
         a2[:, 0:d] = jnp.zeros((8, d), f32)
+        if d == LANES:
+            a3[...] = jnp.zeros((8, d), f32)
+            a4[...] = jnp.zeros((8, d), f32)
 
     def ar_acc(rd, d):
-        ar_go(
-            rd,
-            jnp.sum(a1[:, 0:d], axis=0, keepdims=True),
-            jnp.sum(a2[:, 0:d], axis=0, keepdims=True),
-        )
+        accs = (a1, a2, a3, a4) if d == LANES else (a1, a2)
+        ar_go(rd, [jnp.sum(v[:, 0:d], axis=0, keepdims=True) for v in accs])
 
     def halo(ref):
         d = ref.shape[1]
@@ -263,6 +266,10 @@
             zm = acc * wide(mask[m, pl.ds(base, MT), :], d)
             a1[:, 0:d] += fold(zm)
             a2[:, 0:d] += fold(zm * acc)
+            if layer == last:
+                gy = mask[m, pl.ds(base, MT), :] * grd_p[m, pl.ds(base, MT), :]
+                a3[...] += fold(gy)
+                a4[...] += fold(gy * acc)
 
         ar_acc(rd, d)
 
@@ -298,12 +305,8 @@
 
     def coefs(layer, m, n, g, og, os):
         v1, v2 = ar_get(bround(layer, m), n)
-        if m == 0:
-            og(v2, False)
-            os(v1, False)
-        else:
-            og(v2, True)
-            os(v1, True)
+        og(v2, m > 0)
+        os(v1, m > 0)
         a = g * invs[layer * MB + m, 0:1, 0 : n * LANES]
         return a, a * v1 / cnt[m], a * v2 / cnt[m]
 
@@ -343,9 +346,12 @@
 
         ar_acc(bround(layer - 1, m), chans)
 
+    def gchunk(layer):
+        return GF if layer == 0 else G1 if layer == 1 else chunk(layer)
+
     def wgrad(layer):
         gdrain(layer)
-        w = chunk(layer)
+        w = gchunk(layer)
 
         @pl.loop(0, taps)
         def _(k):
@@ -371,7 +377,7 @@
         return (a.astype(f32) + b.astype(f32)).astype(bf16)
 
     def ra(layer):
-        w = chunk(layer)
+        w = gchunk(layer)
         r0, r1 = rbuf(layer)[0:2]
         wait(r0, r0_r.at[layer])
         for k in range(taps):
@@ -428,9 +434,9 @@
         wait(r3, r3_s.at[layer])
 
     g0(0)
+    g0(1)
     deal(mel_s, mel_r, 0)
-    for c in range(1, last + 1):
-        g0(c)
+    g0(2)
     glp[...] = jnp.zeros(glp.shape, f32)
     slp[...] = jnp.zeros(slp.shape, f32)
     glp[0:1, 0:mels] = gl[...]
@@ -445,89 +451,90 @@
             mask[m, pl.ds(base, ctile), :] = jnp.where(t < own[m], 1.0, 0.0)
 
     g1(0)
+    g2(0)
+    g3(0)
     g1(1)
-    g2(0)
-    g2(1)
-    g3(0)
+
+    @pl.loop(0, utts)
+    def _(u):
+        def body(k, c):
+            return jnp.where(reg_s[rep, k] == u, k, c)
+
+        lens[u] = lax.fori_loop(0, utts, body, jnp.int32(0))
+
     dealt(mel_r, 0)
     for m in range(MB):
         for j in range(n_dp):
             mel_p.at[m][pl.ds(j, frames, stride=SUB), :] = mel_r[j, m].astype(f32)
         h0[m, HALO : HALO + T, :] = (mel_p[m] * mask[m]).astype(bf16)
         halo(h0.at[m])
+        if m == 0:
+            g4(0)
+        conv(0, m)
+        if m == 0:
+            g2(1)
     g1(2)
-    g4(0)
-    conv(0, 0)
-    g3(1)
-    conv(0, 1)
-    g2(2)
-    g4(1)
+    g0(3)
     for layer in range(1, last + 1):
+        g3(layer)
+        g4(layer)
         for m in range(MB):
             norm(layer - 1, m)
+            if layer == last:
+                if m == 0:
+                    dealt(grd_r, 1)
+                for j in range(n_dp):
+                    grd_p.at[m][pl.ds(j, frames, stride=SUB), :] = grd_r[j, m].astype(f32)
             conv(layer, m)
             if m == 0:
+                if layer + 1 <= last:
+                    g2(layer + 1)
+            else:
                 if layer + 2 <= last:
                     g1(layer + 2)
-            else:
-                if layer == 1:
+                if layer + 3 <= last:
+                    g0(layer + 3)
+                if layer == 2:
                     deal(grd_s, grd_r, 1)
-                if layer + 1 <= last:
-                    g3(layer + 1)
-                    if layer + 2 <= last:
-                        g2(layer + 2)
-                    g4(layer + 1)
-
-    dealt(grd_r, 1)
+
     g_last = glp[0:1, :]
     b_last = slp[0:1, :]
+    ct = 64
     for m in range(MB):
-        for j in range(n_dp):
-            grd_p.at[m][pl.ds(j, frames, stride=SUB), :] = grd_r[j, m].astype(f32)
-        mean, inv = mean_inv(last * MB + m, m, 1)
-        clear(LANES)
-        ct = 64
+        tot = ar_get(last * MB + m, 1)
+        mean = tot[0] / cnt[m]
+        var = tot[1] / cnt[m] - mean * mean
+        inv = lax.rsqrt(var + EPS)
+        v1 = tot[2]
+        v2 = inv * (tot[3] - mean * v1)
+        if m == 0:
+            o_gl[...] = v2[:, 0:mels]
+            o_sl[...] = v1[:, 0:mels]
+        else:
+            o_gl[...] = o_gl[...] + v2[:, 0:mels]
+            o_sl[...] = o_sl[...] + v1[:, 0:mels]
+        a = g_last * inv
+        c1 = a * v1 / cnt[m]
+        c2 = a * v2 / cnt[m]
 
         @pl.loop(0, T // ct)
         def _(i):
-            rows = pl.ds(pl.multiple_of(i * ct, ct), ct)
+            base = pl.multiple_of(i * ct, ct)
+            rows = pl.ds(base, ct)
             mk = mask[m, rows, :]
             xv = (zl[m, rows, :] - mean) * inv
-            xl[m, rows, :] = xv
             mel_p[m, rows, :] = mel_p[m, rows, :] + mk * (g_last * xv + b_last)
-            gy = mk * grd_p[m, rows, :]
-            a1[:, 0:LANES] += fold(gy)
-            a2[:, 0:LANES] += fold(gy * xv)
-
-        ar_acc(bround(last, m), LANES)
+            v = a * grd_p[m, rows, :] - c1 - c2 * xv
+            gzl[m, pl.ds(base + HALO, ct), :] = (mk * v).astype(bf16)
+
+        halo(gzl.at[m])
+        grad_h(last, m)
+    wgrad(last)
     for m in range(MB):
         for j in range(n_dp):
             bak_s[j, m] = mel_p.at[m][pl.ds(j, frames, stride=SUB), :].astype(bf16)
     back(bak_s, bak_r, 2)
-    for m in range(MB):
-
-        def og(v, add):
-            v = v[:, 0:mels]
-            o_gl[...] = o_gl[...] + v if add else v
-
-        def os(v, add):
-            v = v[:, 0:mels]
-            o_sl[...] = o_sl[...] + v if add else v
-
-        a, c1, c2 = coefs(last, m, 1, g_last, og, os)
-        ct = 64
-
-        @pl.loop(0, T // ct)
-        def _(i):
-            base = pl.multiple_of(i * ct, ct)
-            rows = pl.ds(base, ct)
-            v = a * grd_p[m, rows, :] - c1 - c2 * xl[m, rows, :]
-            gzl[m, pl.ds(base + HALO, ct), :] = (mask[m, rows, :] * v).astype(bf16)
-
-        halo(gzl.at[m])
-        grad_h(last, m)
-    wgrad(last)
-    for layer in range(middle, 0, -1):
+    for layer in range(middle, 1, -1):
         for m in range(MB):
             grad_z(layer, m)
             grad_h(layer, m)
@@ -535,13 +542,31 @@
                 ra(layer + 1)
                 if layer + 2 <= last:
                     rc(layer + 2)
-            else:
-                rb(layer + 1)
-                if layer + 2 <= last:
-                    rd_(layer + 2)
         wgrad(layer)
+        rb(layer + 1)
+        if layer + 2 <= last:
+            rd_(layer + 2)
+    for m in range(MB):
+        grad_z(1, m)
+    wgrad(1)
+    ra(2)
+    rc(3)
+    grad_h(1, 0)
+    rb(2)
+    rd_(3)
+    grad_h(1, 1)
+    ra(1)
+    backed(bak_r, 2)
+
+    @pl.loop(0, utts)
+    def _(u):
+        o_mel[u] = bak_r[lens[u], :, 0:mels]
+
     for m in range(MB):
         grad_z(0, m)
+    wgrad(0)
+    rc(2)
+    for m in range(MB):
 
         @pl.loop(0, T // MT)
         def _(t):
@@ -554,49 +579,32 @@
             rows = pl.ds(base, MT)
             grd_p[m, rows, :] = grd_p[m, rows, :] + mask[m, rows, :] * acc
 
-        if m == 0:
-            ra(1)
-            rc(2)
         for j in range(n_dp):
             bak2_s[j, m] = grd_p.at[m][pl.ds(j, frames, stride=SUB), :].astype(bf16)
+        if m == 0:
+            rb(1)
+            ra(0)
     back(bak2_s, bak2_r, 3)
-    wgrad(0)
-    rb(1)
-    ra(0)
+    rb(0)
     rd_(2)
-
-    @pl.loop(0, utts)
-    def _(u):
-        def body(k, c):
-            return jnp.where(reg_s[rep, k] == u, k, c)
-
-        lens[u] = lax.fori_loop(0, utts, body, jnp.int32(0))
-
-    backed(bak_r, 2)
-
-    @pl.loop(0, utts)
-    def _(u):
-        o_mel[u] = bak_r[lens[u], :, 0:mels]
-
     rc(1)
-    rb(0)
+    rc(0)
     rd_(1)
-    rc(0)
+    rd_(0)
     backed(bak2_r, 3)
 
     @pl.loop(0, utts)
     def _(u):
         o_grad[u] = bak2_r[lens[u], :, 0:mels]
 
-    rd_(0)
-    for layer in range(last + 1):
+    for layer in reversed(range(last + 1)):
         rdrain(layer)
     wait(mel_r.at[pl.ds(0, n_dp - 1)], a2a_s.at[0])
     wait(grd_r.at[pl.ds(0, n_dp - 1)], a2a_s.at[1])
     wait(bak_r.at[pl.ds(0, utts - MB)], a2a_s.at[2])
     wait(bak2_r.at[pl.ds(0, utts - MB)], a2a_s.at[3])
 
-    @pl.loop(0, 2 * (last + 1) * MB)
+    @pl.loop(0, (2 * last + 1) * MB)
     def _(r):
         wait(ar_r.at[r, pl.ds(0, total - 1)], ars_sem.at[r])
 
@@ -613,7 +621,7 @@
     TH = T + 4 * SUB
     rows = shard // CORES
     total = n_dp * CORES
-    rounds = 2 * depth * MB
+    rounds = (2 * depth - 1) * MB
     V = pltpu.VMEM
     D = pltpu.SemaphoreType.DMA
     S = jax.ShapeDtypeStruct
@@ -645,15 +653,17 @@
         frame_buf, frame_buf, frame_buf2, frame_buf2, frame_buf2, frame_buf2, frame_buf, frame_buf,
         V((MB, T, LANES), f32), V((MB, T, LANES), f32), V((MB, T, LANES), f32),
         V((MB, TH, LANES), bf16), V((middle + 1, MB, TH, chans), bf16),
-        V((middle + 1, MB, T, chans), bf16), V((MB, T, LANES), f32),
+        V((middle + 1, MB, T, chans), bf16),
         V((MB, T, chans), f32), V((MB, T, LANES), f32),
         V((MB, TH, chans), bf16), V((MB, TH, LANES), bf16),
         V((middle, taps, nz, PLANE, CORES, rows, chans), bf16),
         V((taps, nz, PLANE, CORES, rows, LANES), bf16),
         V((taps, nz, PLANE, CORES, rows, LANES), bf16),
+        V((taps, nz, PLANE, CORES, rows, LANES), bf16),
+        V((taps, nz, PLANE, CORES, rows, chans), bf16),
         landing,
         V((rounds, 8, LANES), f32), V((rounds, total, 8, LANES), f32), V((8, LANES), f32),
-        V((8, chans), f32), V((8, chans), f32), V((depth * MB, 8, chans), f32),
+        V((8, chans), f32), V((8, chans), f32), V((8, LANES), f32), V((8, LANES), f32), V((depth * MB, 8, chans), f32),
         V((8, LANES), f32), V((8, LANES), f32), pltpu.SMEM((utts,), jnp.int32),
         D((rounds,)), D((rounds,)), D((4,)), D((4,)),
     ] + [D((depth,))] * 18

time: 253 us -> 218 us (0.86)
  Pallas kernels: 245 us -> 209 us
    pallas_call x1, Pallas kernels: 245 us -> 209 us  [local_kernel(): pl.pallas_call(body, out_shape=out_shape, in_specs=[smem, smem] + [vmem]...]
where the time goes in v2:
time: 218 us
  Pallas kernels  209 us (96%)
  local copies, waits for them, and re-layouts  7.7 us (4%)
    pallas_call x1, Pallas kernels, local_kernel(): pl.pallas_call(body, out_shape=out_shape, in_specs=[smem, smem] + [vmem]...  209 us
    unnamed x25, local copies, waits for them, and re-layouts  7.7 us

profile of v2, /device:TPU:0, one launch (start us, length us, event | category | flops | bytes accessed | tf_op | source)
XLA Modules:
  0.0 217.9 jit_solution(9488116057107188276)
XLA Ops:
  0.6 209.5 %postnet_step.1 = (bf16[32,64,80]{2,1,0:T(8,128)(2,1)}, bf16[32,64,80]{2,1,0:T(8,128)(2,1)}, f32[5,2,16,80]{3,2,1,0:T(8,128)}, f32[3,5,2,16,512]{4,3,2,1,0:T(8,1...) custom-call(s32[64]{0:T(128)} %len_s.1, ...), custom_call_target="tpu_custom_call" | custom-call | tf_op jit(solution)/shard_map/postnet_step/pallas_call | solution.py:673
  210.2 0.0 copy-start.1
  210.2 0.0 copy-start
  210.2 2.0 copy.29
  212.2 0.0 copy-done.1
  212.2 0.0 copy-start.3
  212.2 0.8 copy.30
  213.0 0.1 copy-done.3
  213.1 0.6 copy.31
  213.7 0.0 copy-done
  213.7 0.0 copy-start.2
  213.7 0.9 copy.32
  214.7 0.0 copy-done.2
  214.7 0.0 copy-start.5
  214.7 0.6 copy.33
  215.3 0.1 copy-done.5
  215.4 0.0 copy-start.4
  215.4 0.6 copy.34
  216.0 0.1 copy-done.4
  216.1 0.0 copy-start.7
  216.1 0.6 copy.35
  216.7 0.0 copy-done.7
  216.7 0.0 copy-start.6
  216.7 0.5 copy.36
  217.2 0.2 copy-done.6
  217.4 0.5 copy.37
Async XLA Ops:
  210.2 2.0 copy-start.1
  210.2 3.6 %copy-start = (f32[3,5,2,16,512]{4,3,2,1,0:T(8,128)S(1)}, f32[3,5,2,16,512]{4,3,2,1,0:T(8,128)}, u32[]{:S(2)}) copy-start(f32[3,5,2,16,512]{4,3,2,1,0:T(8,128)} %get-tuple-element.21) | copy-start | bytes 2949124
  212.2 0.9 copy-start.3
  213.7 0.9 copy-start.2
  214.7 0.7 copy-start.5
  215.4 0.7 copy-start.4
  216.1 0.6 copy-start.7
  216.7 0.7 copy-start.6

commit v3 on v2

--- a/solution.py
+++ b/solution.py
@@ -35,10 +35,10 @@
     len_s, reg_s, mel, gpost, wf, wm, wl, gains, shifts, gl, sl,
     o_mel, o_grad, o_wf, o_wm, o_wl, o_gains, o_shifts, o_gl, o_sl,
     mel_s, grd_s, bak_s, bak2_s, mel_r, grd_r, bak_r, bak2_r,
-    mel_p, grd_p, mask, h0, h, xh, z, zl, gz, gzl,
+    whole, pad_m, pad_g, mel_p, grd_p, mask, h0, h, xh, z, zl, gz, gzl,
     W, WF, WL, GF, G1, rbufs,
-    ar_s, ar_r, ar_t, a1, a2, a3, a4, invs, glp, slp, lens,
-    ars_sem, arr_sem, a2a_s, a2a_r, gz_s, gz_r, gp_s, gp_r, gq_s, gq_r, gb_s, gb_r,
+    pl_s, pl_r, z_s, z_r, ar_t, a1, a2, a3, a4, invs, glp, slp, lens,
+    pls_sem, plr_sem, zs_sem, zr_sem, a2a_s, a2a_r, gz_s, gz_r, gp_s, gp_r, gq_s, gq_r, gb_s, gb_r,
     r0_s, r0_r, r1_s, r1_r, r2_s, r2_r, r3_s, r3_r, ro_s, ro_r,
 ):
     nz = n_dp // PLANE
@@ -58,6 +58,8 @@
     s2 = sy + rep * (sx - sy)
     sd = 3 - s
     lin = dp * CORES + rep
+    group = PLANE * CORES
+    mine = s * CORES + rep
     other = 1 - rep
     sib = (dp, other)
     peer1 = (zc * PLANE + s1, rep)
@@ -84,14 +86,48 @@
             barrier, inc=1, device_id=(lax.div(to, CORES), lax.rem(to, CORES)), device_id_type=MESH
         )
 
-    mel_s[...] = jnp.zeros(mel_s.shape, bf16)
-    grd_s[...] = jnp.zeros(grd_s.shape, bf16)
-
-    @pl.loop(0, utts)
-    def _(k):
-        u = reg_s[rep, k]
-        mel_s[k, :, 0:mels] = mel[u]
-        grd_s[k, :, 0:mels] = gpost[u]
+    lane = lax.broadcasted_iota(jnp.int32, (frames, LANES), 1)
+    lane_b = lax.broadcasted_iota(jnp.int32, (SUB, LANES), 1)
+    half = LANES // 2
+    tail = mels - half
+    parts = frames // SUB
+
+    def pack(dst, j, vs):
+        low = jnp.where(lane < half, vs[0], pltpu.roll(vs[1], half, 1))
+        rest = jnp.zeros((SUB, LANES), f32)
+        for m in range(MB):
+            for r in range(parts):
+                at = (m * parts + r) * tail
+                piece = vs[m][r * SUB : (r + 1) * SUB, :]
+                moved = pltpu.roll(piece, (at - half) % LANES, 1) if at != half else piece
+                rest = jnp.where((lane_b >= at) & (lane_b < at + tail), moved, rest)
+        dst[j, 0:frames, :] = low.astype(bf16)
+        dst[j, frames : frames + SUB, :] = rest.astype(bf16)
+
+    def unpack(src, j):
+        low = src[j, 0:frames, :].astype(f32)
+        rest = src[j, frames : frames + SUB, :].astype(f32)
+        vs = []
+        for m in range(MB):
+            pieces = []
+            for r in range(parts):
+                shift = (half - (m * parts + r) * tail) % LANES
+                pieces.append(pltpu.roll(rest, shift, 1) if shift else rest)
+            high = jnp.where(lane < mels, jnp.concatenate(pieces, axis=0), 0.0)
+            vs.append(jnp.where(lane < half, pltpu.roll(low, half, 1) if m else low, high))
+        return vs
+
+    pad_m[...] = jnp.zeros(pad_m.shape, f32)
+    pad_g[...] = jnp.zeros(pad_g.shape, f32)
+
+    def pack_pair(src, pad, dst):
+        @pl.loop(0, n_dp)
+        def _(j):
+            for m in range(MB):
+                pad[m, :, 0:mels] = src[reg_s[rep, j * MB + m]].astype(f32)
+            pack(dst, j, [pad[m] for m in range(MB)])
+
+    pack_pair(mel, pad_m, mel_s)
 
     pl.semaphore_wait(barrier, total - 1)
 
@@ -147,48 +183,64 @@
     def deal(src, dst, which):
         for i in range(1, n_dp):
             to = lax.rem(dp + i, n_dp)
-            send(
-                src.at[pl.ds(to * MB, MB)], dst.at[dp], a2a_s.at[which], a2a_r.at[which], (to, rep)
-            )
-        dst[dp] = src[pl.ds(dp * MB, MB)]
+            send(src.at[to], dst.at[dp], a2a_s.at[which], a2a_r.at[which], (to, rep))
+        dst[dp] = src[dp]
 
     def dealt(dst, which):
         wait(dst.at[pl.ds(0, n_dp - 1)], a2a_r.at[which])
 
-    def back(src, dst, which):
-        for i in range(1, n_dp):
-            to = lax.rem(dp + i, n_dp)
-            send(
-                src.at[to], dst.at[pl.ds(dp * MB, MB)], a2a_s.at[which], a2a_r.at[which], (to, rep)
-            )
-        dst[pl.ds(dp * MB, MB)] = src[dp]
-
-    def backed(dst, which):
-        wait(dst.at[pl.ds(0, utts - MB)], a2a_r.at[which])
+    def spread(src, dst):
+        for j in range(n_dp):
+            for m, v in enumerate(unpack(src, j)):
+                dst.at[m][pl.ds(j, frames, stride=SUB), :] = v
+
+    def collect(src, dst):
+        for j in range(n_dp):
+            pack(dst, j, [src.at[m][pl.ds(j, frames, stride=SUB), :] for m in range(MB)])
+
+    def restore(src, out):
+        for j in range(n_dp):
+            for m, v in enumerate(unpack(src, j)):
+                whole[j * MB + m] = v.astype(bf16)
+
+        @pl.loop(0, utts)
+        def _(u):
+            out[u] = whole[lens[u], :, 0:mels]
 
     def ar_go(rd, vs):
         n = 8 // len(vs)
-        for q, v in enumerate(vs):
+        for e, v in enumerate(vs):
             for i in range(n):
                 if (i + 1) * LANES <= v.shape[1]:
                     row = v[:, i * LANES : (i + 1) * LANES]
                 else:
                     row = jnp.zeros((1, LANES), f32)
-                at = q * n + i
-                ar_s[rd, at : at + 1, :] = row
-                ar_r[rd, lin, at : at + 1, :] = row
-        for i in range(1, total):
-            to = lax.rem(lin + i, total)
+                at = e * n + i
+                pl_s[rd, at : at + 1, :] = row
+                pl_r[rd, mine, at : at + 1, :] = row
+        for i in range(1, group):
+            to = lax.rem(mine + i, group)
             send(
-                ar_s.at[rd], ar_r.at[rd, lin], ars_sem.at[rd], arr_sem.at[rd],
-                (lax.div(to, CORES), lax.rem(to, CORES)),
+                pl_s.at[rd], pl_r.at[rd, mine], pls_sem.at[rd], plr_sem.at[rd],
+                (zc * PLANE + lax.div(to, CORES), lax.rem(to, CORES)),
             )
 
+    def ar_mid(rd):
+        wait(pl_r.at[rd, pl.ds(0, group - 1)], plr_sem.at[rd])
+        acc = pl_r[rd, 0]
+        for i in range(1, group):
+            acc = acc + pl_r[rd, i]
+        z_s[rd] = acc
+        z_r[rd, zc] = acc
+        for i in range(1, nz):
+            to = lax.rem(zc + i, nz) * PLANE + s
+            send(z_s.at[rd], z_r.at[rd, zc], zs_sem.at[rd], zr_sem.at[rd], (to, rep))
+
     def ar_get(rd, n):
-        wait(ar_r.at[rd, pl.ds(0, total - 1)], arr_sem.at[rd])
-        acc = ar_r[rd, 0]
-        for i in range(1, total):
-            acc = acc + ar_r[rd, i]
+        wait(z_r.at[rd, pl.ds(0, nz - 1)], zr_sem.at[rd])
+        acc = z_r[rd, 0]
+        for i in range(1, nz):
+            acc = acc + z_r[rd, i]
         ar_t[...] = acc
         q = CL if n == CL else 2
         return [
@@ -209,7 +261,9 @@
             a3[...] = jnp.zeros((8, d), f32)
             a4[...] = jnp.zeros((8, d), f32)
 
-    def ar_acc(rd, d):
+    def ar_acc(rd, d, before=None):
+        if before is not None:
+            ar_mid(before)
         accs = (a1, a2, a3, a4) if d == LANES else (a1, a2)
         ar_go(rd, [jnp.sum(v[:, 0:d], axis=0, keepdims=True) for v in accs])
 
@@ -271,7 +325,7 @@
                 a3[...] += fold(gy)
                 a4[...] += fold(gy * acc)
 
-        ar_acc(rd, d)
+        ar_acc(rd, d, rd - m if m else None)
 
     def norm(layer, m):
         mean, inv = mean_inv(layer * MB + m, m, CL)
@@ -344,7 +398,7 @@
                 acc = part if acc is None else acc + part
             grad_tail(layer - 1, m, base, acc)
 
-        ar_acc(bround(layer - 1, m), chans)
+        ar_acc(bround(layer - 1, m), chans, bround(layer - 1, 0) if m else None)
 
     def gchunk(layer):
         return GF if layer == 0 else G1 if layer == 1 else chunk(layer)
@@ -457,15 +511,15 @@
 
     @pl.loop(0, utts)
     def _(u):
-        def body(k, c):
-            return jnp.where(reg_s[rep, k] == u, k, c)
-
-        lens[u] = lax.fori_loop(0, utts, body, jnp.int32(0))
-
+        at = jnp.int32(0)
+        for k in range(utts):
+            at = jnp.where(reg_s[rep, k] == u, k, at)
+        lens[u] = at
+
+    pack_pair(gpost, pad_g, grd_s)
     dealt(mel_r, 0)
+    spread(mel_r, mel_p)
     for m in range(MB):
-        for j in range(n_dp):
-            mel_p.at[m][pl.ds(j, frames, stride=SUB), :] = mel_r[j, m].astype(f32)
         h0[m, HALO : HALO + T, :] = (mel_p[m] * mask[m]).astype(bf16)
         halo(h0.at[m])
         if m == 0:
@@ -478,13 +532,12 @@
     for layer in range(1, last + 1):
         g3(layer)
         g4(layer)
+        ar_mid((layer - 1) * MB + 1)
         for m in range(MB):
             norm(layer - 1, m)
-            if layer == last:
-                if m == 0:
-                    dealt(grd_r, 1)
-                for j in range(n_dp):
-                    grd_p.at[m][pl.ds(j, frames, stride=SUB), :] = grd_r[j, m].astype(f32)
+            if layer == last and m == 0:
+                dealt(grd_r, 1)
+                spread(grd_r, grd_p)
             conv(layer, m)
             if m == 0:
                 if layer + 1 <= last:
@@ -497,6 +550,7 @@
                 if layer == 2:
                     deal(grd_s, grd_r, 1)
 
+    ar_mid(last * MB + 1)
     g_last = glp[0:1, :]
     b_last = slp[0:1, :]
     ct = 64
@@ -530,10 +584,9 @@
         halo(gzl.at[m])
         grad_h(last, m)
     wgrad(last)
-    for m in range(MB):
-        for j in range(n_dp):
-            bak_s[j, m] = mel_p.at[m][pl.ds(j, frames, stride=SUB), :].astype(bf16)
-    back(bak_s, bak_r, 2)
+    ar_mid(bround(middle, 1))
+    collect(mel_p, bak_s)
+    deal(bak_s, bak_r, 2)
     for layer in range(middle, 1, -1):
         for m in range(MB):
             grad_z(layer, m)
@@ -543,6 +596,7 @@
                 if layer + 2 <= last:
                     rc(layer + 2)
         wgrad(layer)
+        ar_mid(bround(layer - 1, 1))
         rb(layer + 1)
         if layer + 2 <= last:
             rd_(layer + 2)
@@ -556,11 +610,9 @@
     rd_(3)
     grad_h(1, 1)
     ra(1)
-    backed(bak_r, 2)
-
-    @pl.loop(0, utts)
-    def _(u):
-        o_mel[u] = bak_r[lens[u], :, 0:mels]
+    ar_mid(bround(0, 1))
+    dealt(bak_r, 2)
+    restore(bak_r, o_mel)
 
     for m in range(MB):
         grad_z(0, m)
@@ -579,34 +631,31 @@
             rows = pl.ds(base, MT)
             grd_p[m, rows, :] = grd_p[m, rows, :] + mask[m, rows, :] * acc
 
-        for j in range(n_dp):
-            bak2_s[j, m] = grd_p.at[m][pl.ds(j, frames, stride=SUB), :].astype(bf16)
         if m == 0:
             rb(1)
             ra(0)
-    back(bak2_s, bak2_r, 3)
+    collect(grd_p, bak2_s)
+    deal(bak2_s, bak2_r, 3)
     rb(0)
     rd_(2)
     rc(1)
     rc(0)
     rd_(1)
     rd_(0)
-    backed(bak2_r, 3)
-
-    @pl.loop(0, utts)
-    def _(u):
-        o_grad[u] = bak2_r[lens[u], :, 0:mels]
+    dealt(bak2_r, 3)
+    restore(bak2_r, o_grad)
 
     for layer in reversed(range(last + 1)):
         rdrain(layer)
     wait(mel_r.at[pl.ds(0, n_dp - 1)], a2a_s.at[0])
     wait(grd_r.at[pl.ds(0, n_dp - 1)], a2a_s.at[1])
-    wait(bak_r.at[pl.ds(0, utts - MB)], a2a_s.at[2])
-    wait(bak2_r.at[pl.ds(0, utts - MB)], a2a_s.at[3])
+    wait(bak_r.at[pl.ds(0, n_dp - 1)], a2a_s.at[2])
+    wait(bak2_r.at[pl.ds(0, n_dp - 1)], a2a_s.at[3])
 
     @pl.loop(0, (2 * last + 1) * MB)
     def _(r):
-        wait(ar_r.at[r, pl.ds(0, total - 1)], ars_sem.at[r])
+        wait(pl_r.at[r, pl.ds(0, group - 1)], pls_sem.at[r])
+        wait(z_r.at[r, pl.ds(0, nz - 1)], zs_sem.at[r])
 
 
 def local_kernel(
@@ -620,7 +669,6 @@
     T = n_dp * frames
     TH = T + 4 * SUB
     rows = shard // CORES
-    total = n_dp * CORES
     rounds = (2 * depth - 1) * MB
     V = pltpu.VMEM
     D = pltpu.SemaphoreType.DMA
@@ -636,8 +684,7 @@
         S((1, mels), f32),
         S((1, mels), f32),
     )
-    frame_buf = V((utts, frames, LANES), bf16)
-    frame_buf2 = V((n_dp, MB, frames, LANES), bf16)
+    packed = V((n_dp, frames + SUB, LANES), bf16)
     landing = [
         [
             V((taps, nz, PLANE, rows, d), bf16),
@@ -650,7 +697,8 @@
         for d in [LANES] + [chans] * middle + [LANES]
     ]
     scratch = [
-        frame_buf, frame_buf, frame_buf2, frame_buf2, frame_buf2, frame_buf2, frame_buf, frame_buf,
+        packed, packed, packed, packed, packed, packed, packed, packed,
+        V((utts, frames, LANES), bf16), V((MB, frames, LANES), f32), V((MB, frames, LANES), f32),
         V((MB, T, LANES), f32), V((MB, T, LANES), f32), V((MB, T, LANES), f32),
         V((MB, TH, LANES), bf16), V((middle + 1, MB, TH, chans), bf16),
         V((middle + 1, MB, T, chans), bf16),
@@ -662,10 +710,11 @@
         V((taps, nz, PLANE, CORES, rows, LANES), bf16),
         V((taps, nz, PLANE, CORES, rows, chans), bf16),
         landing,
-        V((rounds, 8, LANES), f32), V((rounds, total, 8, LANES), f32), V((8, LANES), f32),
+        V((rounds, 8, LANES), f32), V((rounds, PLANE * CORES, 8, LANES), f32),
+        V((rounds, 8, LANES), f32), V((rounds, nz, 8, LANES), f32), V((8, LANES), f32),
         V((8, chans), f32), V((8, chans), f32), V((8, LANES), f32), V((8, LANES), f32), V((depth * MB, 8, chans), f32),
         V((8, LANES), f32), V((8, LANES), f32), pltpu.SMEM((utts,), jnp.int32),
-        D((rounds,)), D((rounds,)), D((4,)), D((4,)),
+        D((rounds,)), D((rounds,)), D((rounds,)), D((rounds,)), D((4,)), D((4,)),
     ] + [D((depth,))] * 18
     body = functools.partial(kernel, n_dp, utts, frames, chans, mels, taps, middle)
     vmem = pl.BlockSpec(memory_space=pltpu.VMEM)

time: 218 us -> 211 us (0.968)
  Pallas kernels: 209 us -> 202 us
    pallas_call x1, Pallas kernels: 209 us -> 202 us  [local_kernel(): pl.pallas_call(body, out_shape=out_shape, in_specs=[smem, smem] + [vmem]...]
where the time goes in v3:
time: 211 us
  Pallas kernels  202 us (96%)
  local copies, waits for them, and re-layouts  7.7 us (4%)
    pallas_call x1, Pallas kernels, local_kernel(): pl.pallas_call(body, out_shape=out_shape, in_specs=[smem, smem] + [vmem]...  202 us
    unnamed x25, local copies, waits for them, and re-layouts  7.7 us

profile of v3, /device:TPU:0, one launch (start us, length us, event | category | flops | bytes accessed | tf_op | source)
XLA Modules:
  0.0 210.6 jit_solution(7604402156187994683)
XLA Ops:
  0.6 202.3 %postnet_step.1 = (bf16[32,64,80]{2,1,0:T(8,128)(2,1)}, bf16[32,64,80]{2,1,0:T(8,128)(2,1)}, f32[5,2,16,80]{3,2,1,0:T(8,128)}, f32[3,5,2,16,512]{4,3,2,1,0:T(8,1...) custom-call(s32[64]{0:T(128)} %len_s.1, ...), custom_call_target="tpu_custom_call" | custom-call | tf_op jit(solution)/shard_map/postnet_step/pallas_call | solution.py:722
  202.9 0.0 copy-start.1
  202.9 0.0 copy-start
  202.9 2.0 copy.29
  204.9 0.0 copy-done.1
  204.9 0.0 copy-start.3
  204.9 0.8 copy.30
  205.7 0.1 copy-done.3
  205.8 0.6 copy.31
  206.5 0.0 copy-done
  206.5 0.0 copy-start.2
  206.5 0.9 copy.32
  207.4 0.0 copy-done.2
  207.4 0.0 copy-start.5
  207.4 0.6 copy.33
  208.1 0.1 copy-done.5
  208.1 0.0 copy-start.4
  208.1 0.6 copy.34
  208.7 0.1 copy-done.4
  208.8 0.0 copy-start.7
  208.8 0.6 copy.35
  209.4 0.0 copy-done.7
  209.4 0.0 copy-start.6
  209.4 0.5 copy.36
  210.0 0.2 copy-done.6
  210.1 0.5 copy.37
Async XLA Ops:
  202.9 2.0 copy-start.1
  202.9 3.6 %copy-start = (f32[3,5,2,16,512]{4,3,2,1,0:T(8,128)S(1)}, f32[3,5,2,16,512]{4,3,2,1,0:T(8,128)}, u32[]{:S(2)}) copy-start(f32[3,5,2,16,512]{4,3,2,1,0:T(8,128)} %get-tuple-element.21) | copy-start | bytes 2949124
  204.9 0.9 copy-start.3
  206.5 0.9 copy-start.2
  207.4 0.7 copy-start.5
  208.1 0.7 copy-start.4
  208.8 0.6 copy-start.7
  209.4 0.7 copy-start.6

commit v4 on v3

--- a/solution.py
+++ b/solution.py
@@ -37,8 +37,8 @@
     mel_s, grd_s, bak_s, bak2_s, mel_r, grd_r, bak_r, bak2_r,
     whole, pad_m, pad_g, mel_p, grd_p, mask, h0, h, xh, z, zl, gz, gzl,
     W, WF, WL, GF, G1, rbufs,
-    pl_s, pl_r, z_s, z_r, ar_t, a1, a2, a3, a4, invs, glp, slp, lens,
-    pls_sem, plr_sem, zs_sem, zr_sem, a2a_s, a2a_r, gz_s, gz_r, gp_s, gp_r, gq_s, gq_r, gb_s, gb_r,
+    dr_s, dr_r, pl_s, pl_r, z_s, z_r, ar_t, a1, a2, a3, a4, invs, glp, slp, lens,
+    drs_sem, drr_sem, pls_sem, plr_sem, zs_sem, zr_sem, a2a_s, a2a_r, gz_s, gz_r, gp_s, gp_r, gq_s, gq_r, gb_s, gb_r,
     r0_s, r0_r, r1_s, r1_r, r2_s, r2_r, r3_s, r3_r, ro_s, ro_r,
 ):
     nz = n_dp // PLANE
@@ -47,7 +47,7 @@
     HALO = 2 * SUB
     MT = T // 2
     CL = chans // LANES
-    ctile = 32
+    ctile = 64
     dp = lax.axis_index("dp")
     rep = lax.axis_index("rep")
     zc = lax.div(dp, PLANE)
@@ -138,47 +138,64 @@
             return WL
         return W.at[c - 1]
 
-    def g0(c):
-        w = chunk(c)
+    units = []
+    for layer in range(middle + 2):
+        cuts = (0, 2, taps) if layer == 1 else (0, taps)
+        units += [(layer, k0, k1) for k0, k1 in zip(cuts[:-1], cuts[1:])]
+
+    def parts_of(c):
+        return [
+            (u, chunk(c).at[pl.ds(k0, k1 - k0)])
+            for u, (layer, k0, k1) in enumerate(units)
+            if layer == c
+        ]
+
+    def three(w):
+        return w.at[:, pl.ds(0, nz - 1), 0, 0]
+
+    def g0u(u, w):
         for i in range(1, nz):
             to = lax.rem(zc + i, nz) * PLANE + s
             piece = w.at[:, zc, s, rep]
-            send(piece, piece, gz_s.at[c], gz_r.at[c], (to, rep))
-
-    def three(w):
-        return w.at[:, pl.ds(0, nz - 1), 0, 0]
-
-    def g1(c):
-        w = chunk(c)
-        wait(three(w), gz_r.at[c])
+            send(piece, piece, gz_s.at[u], gz_r.at[u], (to, rep))
+
+    def g1u(u, w):
+        wait(three(w), gz_r.at[u])
         col = w.at[:, :, s, rep]
-        send(col, col, gp_s.at[c], gp_r.at[c], peer1)
-        send(col, col, gq_s.at[c], gq_r.at[c], peer2)
-        send(col, col, gb_s.at[c], gb_r.at[c], sib)
-
-    def g2(c):
-        w = chunk(c)
-        wait(w.at[:, :, 0, 0], gp_r.at[c])
+        send(col, col, gp_s.at[u], gp_r.at[u], peer1)
+        send(col, col, gq_s.at[u], gq_r.at[u], peer2)
+        send(col, col, gb_s.at[u], gb_r.at[u], sib)
+
+    def g2u(u, w):
+        wait(w.at[:, :, 0, 0], gp_r.at[u])
         col = w.at[:, :, s1, rep]
-        send(col, col, gq_s.at[c], gq_r.at[c], peer2)
-        send(col, col, gb_s.at[c], gb_r.at[c], sib)
-
-    def g3(c):
-        w = chunk(c)
-        wait(w.at[:, :, pl.ds(0, 2), 0], gq_r.at[c])
+        send(col, col, gq_s.at[u], gq_r.at[u], peer2)
+        send(col, col, gb_s.at[u], gb_r.at[u], sib)
+
+    def g3u(u, w):
+        wait(w.at[:, :, pl.ds(0, 2), 0], gq_r.at[u])
         for q in (s2, sd):
             col = w.at[:, :, q, rep]
-            send(col, col, gb_s.at[c], gb_r.at[c], sib)
-
-    def g4(c):
-        wait(chunk(c).at[:, :, :, 0], gb_r.at[c])
-
-    def gdrain(c):
-        w = chunk(c)
-        wait(three(w), gz_s.at[c])
-        wait(w.at[:, :, 0, 0], gp_s.at[c])
-        wait(w.at[:, :, pl.ds(0, 2), 0], gq_s.at[c])
-        wait(w.at[:, :, :, 0], gb_s.at[c])
+            send(col, col, gb_s.at[u], gb_r.at[u], sib)
+
+    def g4u(u, w):
+        wait(w.at[:, :, :, 0], gb_r.at[u])
+
+    def gdrainu(u, w):
+        wait(three(w), gz_s.at[u])
+        wait(w.at[:, :, 0, 0], gp_s.at[u])
+        wait(w.at[:, :, pl.ds(0, 2), 0], gq_s.at[u])
+        wait(w.at[:, :, :, 0], gb_s.at[u])
+
+    def each(fn):
+        def run(c, only=None):
+            for i, (u, w) in enumerate(parts_of(c)):
+                if only is None or i == only:
+                    fn(u, w)
+
+        return run
+
+    g0, g1, g2, g3, g4, gdrain = [each(f) for f in (g0u, g1u, g2u, g3u, g4u, gdrainu)]
 
     def deal(src, dst, which):
         for i in range(1, n_dp):
@@ -207,8 +224,14 @@
         def _(u):
             out[u] = whole[lens[u], :, 0:mels]
 
+    direct = (middle + 2) * MB
+
     def ar_go(rd, vs):
         n = 8 // len(vs)
+        if rd < direct:
+            src, dst, slot = dr_s.at[rd], dr_r.at[rd], lin
+        else:
+            src, dst, slot = pl_s.at[rd - direct], pl_r.at[rd - direct], mine
         for e, v in enumerate(vs):
             for i in range(n):
                 if (i + 1) * LANES <= v.shape[1]:
@@ -216,16 +239,27 @@
                 else:
                     row = jnp.zeros((1, LANES), f32)
                 at = e * n + i
-                pl_s[rd, at : at + 1, :] = row
-                pl_r[rd, mine, at : at + 1, :] = row
+                src[at : at + 1, :] = row
+                dst[slot, at : at + 1, :] = row
+        if rd < direct:
+            for i in range(1, total):
+                to = lax.rem(lin + i, total)
+                send(
+                    src, dst.at[lin], drs_sem.at[rd], drr_sem.at[rd],
+                    (lax.div(to, CORES), lax.rem(to, CORES)),
+                )
+            return
         for i in range(1, group):
             to = lax.rem(mine + i, group)
             send(
-                pl_s.at[rd], pl_r.at[rd, mine], pls_sem.at[rd], plr_sem.at[rd],
+                src, dst.at[mine], pls_sem.at[rd - direct], plr_sem.at[rd - direct],
                 (zc * PLANE + lax.div(to, CORES), lax.rem(to, CORES)),
             )
 
     def ar_mid(rd):
+        if rd < direct:
+            return
+        rd = rd - direct
         wait(pl_r.at[rd, pl.ds(0, group - 1)], plr_sem.at[rd])
         acc = pl_r[rd, 0]
         for i in range(1, group):
@@ -237,10 +271,16 @@
             send(z_s.at[rd], z_r.at[rd, zc], zs_sem.at[rd], zr_sem.at[rd], (to, rep))
 
     def ar_get(rd, n):
-        wait(z_r.at[rd, pl.ds(0, nz - 1)], zr_sem.at[rd])
-        acc = z_r[rd, 0]
-        for i in range(1, nz):
-            acc = acc + z_r[rd, i]
+        if rd < direct:
+            wait(dr_r.at[rd, pl.ds(0, total - 1)], drr_sem.at[rd])
+            acc = dr_r[rd, 0]
+            for i in range(1, total):
+                acc = acc + dr_r[rd, i]
+        else:
+            wait(z_r.at[rd - direct, pl.ds(0, nz - 1)], zr_sem.at[rd - direct])
+            acc = z_r[rd - direct, 0]
+            for i in range(1, nz):
+                acc = acc + z_r[rd - direct, i]
         ar_t[...] = acc
         q = CL if n == CL else 2
         return [
@@ -297,6 +337,11 @@
         invs[rd, 0:1, 0 : n * LANES] = inv
         return mean, inv
 
+    pairs = [tuple(range(k, min(k + 2, taps))) for k in range(0, taps, 2)]
+
+    def joined(vs):
+        return jnp.concatenate(vs, axis=1) if len(vs) > 1 else vs[0]
+
     def conv(layer, m):
         rd = layer * MB + m
         d = LANES if layer == last else chans
@@ -307,15 +352,21 @@
         def _(t):
             base = pl.multiple_of(t * MT, MT)
             acc = None
-            for k in range(taps):
-                rows = pl.ds(base + SUB * k, MT)
-                if layer == 0:
-                    part = nt(h0[m, rows, :], WF[k].reshape(chans, LANES))
-                elif layer == last:
-                    part = nn(h[layer - 1, m, rows, :], WL[k].reshape(chans, LANES))
-                else:
-                    part = nn(h[layer - 1, m, rows, :], W[layer - 1, k].reshape(chans, chans))
-                acc = part if acc is None else acc + part
+            if layer == 0:
+                for ks in pairs:
+                    prod = nt(
+                        joined([h0[m, pl.ds(base + SUB * k, MT), :] for k in ks]),
+                        joined([WF[k].reshape(chans, LANES) for k in ks]),
+                    )
+                    acc = prod if acc is None else acc + prod
+            else:
+                for k in range(taps):
+                    rows = pl.ds(base + SUB * k, MT)
+                    if layer == last:
+                        prod = nn(h[layer - 1, m, rows, :], WL[k].reshape(chans, LANES))
+                    else:
+                        prod = nn(h[layer - 1, m, rows, :], W[layer - 1, k].reshape(chans, chans))
+                    acc = prod if acc is None else acc + prod
             dst[m, pl.ds(base, MT), :] = acc
             zm = acc * wide(mask[m, pl.ds(base, MT), :], d)
             a1[:, 0:d] += fold(zm)
@@ -389,13 +440,18 @@
         def _(t):
             base = pl.multiple_of(t * MT, MT)
             acc = None
-            for k in range(taps):
-                rows = pl.ds(base + SUB * (taps - 1 - k), MT)
-                if layer == last:
-                    part = nt(gzl[m, rows, :], WL[k].reshape(chans, LANES))
-                else:
-                    part = nt(gz[m, rows, :], W[layer - 1, k].reshape(chans, chans))
-                acc = part if acc is None else acc + part
+            if layer == last:
+                for ks in pairs:
+                    prod = nt(
+                        joined([gzl[m, pl.ds(base + SUB * (taps - 1 - k), MT), :] for k in ks]),
+                        joined([WL[k].reshape(chans, LANES) for k in ks]),
+                    )
+                    acc = prod if acc is None else acc + prod
+            else:
+                for k in range(taps):
+                    rows = pl.ds(base + SUB * (taps - 1 - k), MT)
+                    prod = nt(gz[m, rows, :], W[layer - 1, k].reshape(chans, chans))
+                    acc = prod if acc is None else acc + prod
             grad_tail(layer - 1, m, base, acc)
 
         ar_acc(bround(layer - 1, m), chans, bround(layer - 1, 0) if m else None)
@@ -403,25 +459,40 @@
     def gchunk(layer):
         return GF if layer == 0 else G1 if layer == 1 else chunk(layer)
 
-    def wgrad(layer):
+    def wgrad(layer, split=0, between=()):
         gdrain(layer)
         w = gchunk(layer)
 
-        @pl.loop(0, taps)
-        def _(k):
-            if layer == 0:
-                rows = pl.ds(pl.multiple_of(SUB * k, SUB), T)
-                acc = tn(gz[0, HALO : HALO + T, :], h0[0, rows, :])
-                for m in range(1, MB):
-                    acc = acc + tn(gz[m, HALO : HALO + T, :], h0[m, rows, :])
-            else:
-                g = gzl if layer == last else gz
-                rows = pl.ds(pl.multiple_of(SUB * (taps - 1 - k), SUB), T)
-                acc = tn(h[layer - 1, 0, HALO : HALO + T, :], g[0, rows, :])
-                for m in range(1, MB):
-                    acc = acc + tn(h[layer - 1, m, HALO : HALO + T, :], g[m, rows, :])
+        def narrow(ks):
+            acc = None
+            for m in range(MB):
+                if layer == 0:
+                    right = joined([h0[m, pl.ds(SUB * k, T), :] for k in ks])
+                    prod = tn(gz[m, HALO : HALO + T, :], right)
+                else:
+                    right = joined([gzl[m, pl.ds(SUB * (taps - 1 - k), T), :] for k in ks])
+                    prod = tn(h[layer - 1, m, HALO : HALO + T, :], right)
+                acc = prod if acc is None else acc + prod
+            for i, k in enumerate(ks):
+                v = acc[:, i * LANES : (i + 1) * LANES]
+                w[k] = v.astype(bf16).reshape(w.shape[1:])
+
+        def one(k):
+            rows = pl.ds(pl.multiple_of(SUB * (taps - 1 - k), SUB), T)
+            acc = tn(h[layer - 1, 0, HALO : HALO + T, :], gz[0, rows, :])
+            for m in range(1, MB):
+                acc = acc + tn(h[layer - 1, m, HALO : HALO + T, :], gz[m, rows, :])
             w[k] = acc.astype(bf16).reshape(w.shape[1:])
 
+        if layer in (0, last):
+            for ks in pairs:
+                narrow(ks)
+        else:
+            if split:
+                pl.loop(0, split)(one)
+                for fn, arg in between:
+                    fn(arg)
+            pl.loop(split, taps)(one)
         send(w.at[:, :, :, other], rbuf(layer)[0], r0_s.at[layer], r0_r.at[layer], sib)
 
     def rbuf(layer):
@@ -505,9 +576,11 @@
             mask[m, pl.ds(base, ctile), :] = jnp.where(t < own[m], 1.0, 0.0)
 
     g1(0)
+    g1(1, 0)
     g2(0)
+    g1(1, 1)
     g3(0)
-    g1(1)
+    g2(1, 0)
 
     @pl.loop(0, utts)
     def _(u):
@@ -524,15 +597,16 @@
         halo(h0.at[m])
         if m == 0:
             g4(0)
+        if m == 0:
+            g2(1, 1)
+            g3(1, 0)
         conv(0, m)
-        if m == 0:
-            g2(1)
     g1(2)
     g0(3)
     for layer in range(1, last + 1):
-        g3(layer)
+        ar_mid((layer - 1) * MB + 1)
+        g3(layer, 1 if layer == 1 else None)
         g4(layer)
-        ar_mid((layer - 1) * MB + 1)
         for m in range(MB):
             norm(layer - 1, m)
             if layer == last and m == 0:
@@ -584,8 +658,8 @@
         halo(gzl.at[m])
         grad_h(last, m)
     wgrad(last)
+    collect(mel_p, bak_s)
     ar_mid(bround(middle, 1))
-    collect(mel_p, bak_s)
     deal(bak_s, bak_r, 2)
     for layer in range(middle, 1, -1):
         for m in range(MB):
@@ -593,31 +667,28 @@
             grad_h(layer, m)
             if m == 0:
                 ra(layer + 1)
-                if layer + 2 <= last:
-                    rc(layer + 2)
-        wgrad(layer)
-        ar_mid(bround(layer - 1, 1))
-        rb(layer + 1)
-        if layer + 2 <= last:
-            rd_(layer + 2)
+        mid = (ar_mid, bround(layer - 1, 1))
+        if layer + 1 == last:
+            rb(layer + 1)
+            wgrad(layer, 3, (mid, (rc, layer + 1)))
+            rd_(layer + 1)
+        else:
+            wgrad(layer, 3, (mid, (rb, layer + 1)))
     for m in range(MB):
         grad_z(1, m)
-    wgrad(1)
-    ra(2)
-    rc(3)
+    wgrad(1, 2, ((rc, 3), (ra, 2)) if middle > 2 else ())
     grad_h(1, 0)
     rb(2)
     rd_(3)
     grad_h(1, 1)
     ra(1)
-    ar_mid(bround(0, 1))
     dealt(bak_r, 2)
     restore(bak_r, o_mel)
-
+    ar_mid(bround(0, 1))
+    rc(2)
     for m in range(MB):
         grad_z(0, m)
     wgrad(0)
-    rc(2)
     for m in range(MB):
 
         @pl.loop(0, T // MT)
@@ -631,20 +702,18 @@
             rows = pl.ds(base, MT)
             grd_p[m, rows, :] = grd_p[m, rows, :] + mask[m, rows, :] * acc
 
-        if m == 0:
-            rb(1)
-            ra(0)
+    rb(1)
     collect(grd_p, bak2_s)
     deal(bak2_s, bak2_r, 3)
-    rb(0)
+    ra(0)
     rd_(2)
     rc(1)
+    rb(0)
     rc(0)
+    dealt(bak2_r, 3)
+    restore(bak2_r, o_grad)
     rd_(1)
     rd_(0)
-    dealt(bak2_r, 3)
-    restore(bak2_r, o_grad)
-
     for layer in reversed(range(last + 1)):
         rdrain(layer)
     wait(mel_r.at[pl.ds(0, n_dp - 1)], a2a_s.at[0])
@@ -652,7 +721,11 @@
     wait(bak_r.at[pl.ds(0, n_dp - 1)], a2a_s.at[2])
     wait(bak2_r.at[pl.ds(0, n_dp - 1)], a2a_s.at[3])
 
-    @pl.loop(0, (2 * last + 1) * MB)
+    @pl.loop(0, direct)
+    def _(r):
+        wait(dr_r.at[r, pl.ds(0, total - 1)], drs_sem.at[r])
+
+    @pl.loop(0, last * MB)
     def _(r):
         wait(pl_r.at[r, pl.ds(0, group - 1)], pls_sem.at[r])
         wait(z_r.at[r, pl.ds(0, nz - 1)], zs_sem.at[r])
@@ -669,7 +742,8 @@
     T = n_dp * frames
     TH = T + 4 * SUB
     rows = shard // CORES
-    rounds = (2 * depth - 1) * MB
+    direct = depth * MB
+    rounds = (depth - 1) * MB
     V = pltpu.VMEM
     D = pltpu.SemaphoreType.DMA
     S = jax.ShapeDtypeStruct
@@ -710,12 +784,14 @@
         V((taps, nz, PLANE, CORES, rows, LANES), bf16),
         V((taps, nz, PLANE, CORES, rows, chans), bf16),
         landing,
+        V((direct, 8, LANES), f32), V((direct, n_dp * CORES, 8, LANES), f32),
         V((rounds, 8, LANES), f32), V((rounds, PLANE * CORES, 8, LANES), f32),
         V((rounds, 8, LANES), f32), V((rounds, nz, 8, LANES), f32), V((8, LANES), f32),
         V((8, chans), f32), V((8, chans), f32), V((8, LANES), f32), V((8, LANES), f32), V((depth * MB, 8, chans), f32),
         V((8, LANES), f32), V((8, LANES), f32), pltpu.SMEM((utts,), jnp.int32),
+        D((direct,)), D((direct,)),
         D((rounds,)), D((rounds,)), D((rounds,)), D((rounds,)), D((4,)), D((4,)),
-    ] + [D((depth,))] * 18
+    ] + [D((depth + 1,))] * 18
     body = functools.partial(kernel, n_dp, utts, frames, chans, mels, taps, middle)
     vmem = pl.BlockSpec(memory_space=pltpu.VMEM)
     smem = pl.BlockSpec(memory_space=pltpu.SMEM)

time: 211 us -> 201 us (0.953)
  Pallas kernels: 202 us -> 192 us
    pallas_call x1, Pallas kernels: 202 us -> 192 us  [local_kernel(): pl.pallas_call(body, out_shape=out_shape, in_specs=[smem, smem] + [vmem]...]
where the time goes in v4:
time: 201 us
  Pallas kernels  192 us (96%)
  local copies, waits for them, and re-layouts  7.7 us (4%)
    pallas_call x1, Pallas kernels, local_kernel(): pl.pallas_call(body, out_shape=out_shape, in_specs=[smem, smem] + [vmem]...  192 us
    unnamed x25, local copies, waits for them, and re-layouts  7.7 us

profile of v4, /device:TPU:0, one launch (start us, length us, event | category | flops | bytes accessed | tf_op | source)
XLA Modules:
  0.0 200.9 jit_solution(16541571965122721356)
XLA Ops:
  0.6 192.5 %postnet_step.1 = (bf16[32,64,80]{2,1,0:T(8,128)(2,1)}, bf16[32,64,80]{2,1,0:T(8,128)(2,1)}, f32[5,2,16,80]{3,2,1,0:T(8,128)}, f32[3,5,2,16,512]{4,3,2,1,0:T(8,1...) custom-call(s32[64]{0:T(128)} %len_s.1, ...), custom_call_target="tpu_custom_call" | custom-call | tf_op jit(solution)/shard_map/postnet_step/pallas_call | solution.py:798
  193.1 0.0 copy-start.1
  193.1 0.0 copy-start
  193.2 2.0 copy.29
  195.1 0.0 copy-done.1
  195.1 0.0 copy-start.3
  195.1 0.8 copy.30
  195.9 0.1 copy-done.3
  196.1 0.6 copy.31
  196.7 0.0 copy-done
  196.7 0.0 copy-start.2
  196.7 0.9 copy.32
  197.7 0.0 copy-done.2
  197.7 0.0 copy-start.5
  197.7 0.6 copy.33
  198.3 0.1 copy-done.5
  198.4 0.0 copy-start.4
  198.4 0.6 copy.34
  199.0 0.1 copy-done.4
  199.1 0.0 copy-start.7
  199.1 0.6 copy.35
  199.7 0.0 copy-done.7
  199.7 0.0 copy-start.6
  199.7 0.5 copy.36
  200.2 0.2 copy-done.6
  200.3 0.5 copy.37
Async XLA Ops:
  193.1 2.0 copy-start.1
  193.1 3.6 %copy-start = (f32[3,5,2,16,512]{4,3,2,1,0:T(8,128)S(1)}, f32[3,5,2,16,512]{4,3,2,1,0:T(8,128)}, u32[]{:S(2)}) copy-start(f32[3,5,2,16,512]{4,3,2,1,0:T(8,128)} %get-tuple-element.21) | copy-start | bytes 2949124
  195.1 0.9 copy-start.3
  196.7 0.9 copy-start.2
  197.7 0.7 copy-start.5
  198.4 0.7 copy-start.4
  199.1 0.6 copy-start.7
  199.7 0.7 copy-start.6

commit v5 on v4

--- a/solution.py
+++ b/solution.py
@@ -224,14 +224,20 @@
         def _(u):
             out[u] = whole[lens[u], :, 0:mels]
 
-    direct = (middle + 2) * MB
+    all_rounds = (2 * (middle + 2) - 1) * MB
+    exposed = [(middle + 2) * MB + m for m in range(MB)]
+    exposed += [(middle + 2 + middle) * MB + m for m in range(MB)]
+    straight = list(range((middle + 2) * MB)) + exposed
+    stepped = [r for r in range(all_rounds) if r not in straight]
 
     def ar_go(rd, vs):
         n = 8 // len(vs)
-        if rd < direct:
+        plain = rd in straight
+        rd = straight.index(rd) if plain else stepped.index(rd)
+        if plain:
             src, dst, slot = dr_s.at[rd], dr_r.at[rd], lin
         else:
-            src, dst, slot = pl_s.at[rd - direct], pl_r.at[rd - direct], mine
+            src, dst, slot = pl_s.at[rd], pl_r.at[rd], mine
         for e, v in enumerate(vs):
             for i in range(n):
                 if (i + 1) * LANES <= v.shape[1]:
@@ -241,7 +247,7 @@
                 at = e * n + i
                 src[at : at + 1, :] = row
                 dst[slot, at : at + 1, :] = row
-        if rd < direct:
+        if plain:
             for i in range(1, total):
                 to = lax.rem(lin + i, total)
                 send(
@@ -252,14 +258,14 @@
         for i in range(1, group):
             to = lax.rem(mine + i, group)
             send(
-                src, dst.at[mine], pls_sem.at[rd - direct], plr_sem.at[rd - direct],
+                src, dst.at[mine], pls_sem.at[rd], plr_sem.at[rd],
                 (zc * PLANE + lax.div(to, CORES), lax.rem(to, CORES)),
             )
 
     def ar_mid(rd):
-        if rd < direct:
+        if rd in straight:
             return
-        rd = rd - direct
+        rd = stepped.index(rd)
         wait(pl_r.at[rd, pl.ds(0, group - 1)], plr_sem.at[rd])
         acc = pl_r[rd, 0]
         for i in range(1, group):
@@ -271,16 +277,18 @@
             send(z_s.at[rd], z_r.at[rd, zc], zs_sem.at[rd], zr_sem.at[rd], (to, rep))
 
     def ar_get(rd, n):
-        if rd < direct:
+        if rd in straight:
+            rd = straight.index(rd)
             wait(dr_r.at[rd, pl.ds(0, total - 1)], drr_sem.at[rd])
             acc = dr_r[rd, 0]
             for i in range(1, total):
                 acc = acc + dr_r[rd, i]
         else:
-            wait(z_r.at[rd - direct, pl.ds(0, nz - 1)], zr_sem.at[rd - direct])
-            acc = z_r[rd - direct, 0]
+            rd = stepped.index(rd)
+            wait(z_r.at[rd, pl.ds(0, nz - 1)], zr_sem.at[rd])
+            acc = z_r[rd, 0]
             for i in range(1, nz):
-                acc = acc + z_r[rd - direct, i]
+                acc = acc + z_r[rd, i]
         ar_t[...] = acc
         q = CL if n == CL else 2
         return [
@@ -721,11 +729,11 @@
     wait(bak_r.at[pl.ds(0, n_dp - 1)], a2a_s.at[2])
     wait(bak2_r.at[pl.ds(0, n_dp - 1)], a2a_s.at[3])
 
-    @pl.loop(0, direct)
+    @pl.loop(0, len(straight))
     def _(r):
         wait(dr_r.at[r, pl.ds(0, total - 1)], drs_sem.at[r])
 
-    @pl.loop(0, last * MB)
+    @pl.loop(0, len(stepped))
     def _(r):
         wait(pl_r.at[r, pl.ds(0, group - 1)], pls_sem.at[r])
         wait(z_r.at[r, pl.ds(0, nz - 1)], zs_sem.at[r])
@@ -742,8 +750,8 @@
     T = n_dp * frames
     TH = T + 4 * SUB
     rows = shard // CORES
-    direct = depth * MB
-    rounds = (depth - 1) * MB
+    direct = (depth + 2) * MB
+    rounds = (depth - 3) * MB
     V = pltpu.VMEM
     D = pltpu.SemaphoreType.DMA
     S = jax.ShapeDtypeStruct

time: 201 us -> 198 us (0.985)
  Pallas kernels: 192 us -> 189 us
    pallas_call x1, Pallas kernels: 192 us -> 189 us  [local_kernel(): pl.pallas_call(body, out_shape=out_shape, in_specs=[smem, smem] + [vmem]...]
where the time goes in v5:
time: 198 us
  Pallas kernels  189 us (95%)
  local copies, waits for them, and re-layouts  7.7 us (4%)
    pallas_call x1, Pallas kernels, local_kernel(): pl.pallas_call(body, out_shape=out_shape, in_specs=[smem, smem] + [vmem]...  189 us
    unnamed x25, local copies, waits for them, and re-layouts  7.7 us

profile of v5, /device:TPU:0, one launch (start us, length us, event | category | flops | bytes accessed | tf_op | source)
XLA Modules:
  0.0 197.7 jit_solution(13264617075737487760)
XLA Ops:
  0.6 189.3 %postnet_step.1 = (bf16[32,64,80]{2,1,0:T(8,128)(2,1)}, bf16[32,64,80]{2,1,0:T(8,128)(2,1)}, f32[5,2,16,80]{3,2,1,0:T(8,128)}, f32[3,5,2,16,512]{4,3,2,1,0:T(8,1...) custom-call(s32[64]{0:T(128)} %len_s.1, ...), custom_call_target="tpu_custom_call" | custom-call | tf_op jit(solution)/shard_map/postnet_step/pallas_call | solution.py:806
  189.9 0.0 copy-start.1
  189.9 0.0 copy-start
  190.0 2.0 %copy.29 = bf16[32,64,80]{2,1,0:T(8,128)(2,1)} copy(bf16[32,64,80]{2,1,0:T(8,128)(2,1)} %get-tuple-element.36) | data formatting | bytes 655360
  191.9 0.0 copy-done.1
  191.9 0.0 copy-start.3
  191.9 0.8 copy.30
  192.7 0.1 copy-done.3
  192.9 0.6 copy.31
  193.5 0.0 copy-done
  193.5 0.0 copy-start.2
  193.5 0.9 copy.32
  194.5 0.0 copy-done.2
  194.5 0.0 copy-start.5
  194.5 0.6 copy.33
  195.1 0.1 copy-done.5
  195.2 0.0 copy-start.4
  195.2 0.6 copy.34
  195.8 0.1 copy-done.4
  195.9 0.0 copy-start.7
  195.9 0.6 copy.35
  196.5 0.0 copy-done.7
  196.5 0.0 copy-start.6
  196.5 0.5 copy.36
  197.0 0.2 copy-done.6
  197.1 0.5 copy.37
Async XLA Ops:
  189.9 2.0 %copy-start.1 = (bf16[32,64,80]{2,1,0:T(8,128)(2,1)S(1)}, bf16[32,64,80]{2,1,0:T(8,128)(2,1)}, u32[]{:S(2)}) copy-start(bf16[32,64,80]{2,1,0:T(8,128)(2,1)} %get-tuple-element.37) | copy-start | bytes 983044
  189.9 3.6 %copy-start = (f32[3,5,2,16,512]{4,3,2,1,0:T(8,128)S(1)}, f32[3,5,2,16,512]{4,3,2,1,0:T(8,128)}, u32[]{:S(2)}) copy-start(f32[3,5,2,16,512]{4,3,2,1,0:T(8,128)} %get-tuple-element.21) | copy-start | bytes 2949124
  191.9 0.9 copy-start.3
  193.5 0.9 copy-start.2
  194.5 0.7 copy-start.5
  195.2 0.7 copy-start.4
  195.9 0.6 copy-start.7
  196.5 0.7 copy-start.6

commit v6 on v5

--- a/solution.py
+++ b/solution.py
@@ -127,8 +127,6 @@
                 pad[m, :, 0:mels] = src[reg_s[rep, j * MB + m]].astype(f32)
             pack(dst, j, [pad[m] for m in range(MB)])
 
-    pack_pair(mel, pad_m, mel_s)
-
     pl.semaphore_wait(barrier, total - 1)
 
     def chunk(c):
@@ -568,6 +566,7 @@
 
     g0(0)
     g0(1)
+    pack_pair(mel, pad_m, mel_s)
     deal(mel_s, mel_r, 0)
     g0(2)
     glp[...] = jnp.zeros(glp.shape, f32)

time: 198 us -> 198 us (level)
  no operation moved by 1% of the time
where the time goes in v6:
time: 198 us; the launch traced here: 197 us
  Pallas kernels  189 us (95%)
  local copies, waits for them, and re-layouts  7.7 us (4%)
    pallas_call x1, Pallas kernels, local_kernel(): pl.pallas_call(body, out_shape=out_shape, in_specs=[smem, smem] + [vmem]...  189 us
    unnamed x25, local copies, waits for them, and re-layouts  7.7 us

profile of v6, /device:TPU:0, one launch (start us, length us, event | category | flops | bytes accessed | tf_op | source)
XLA Modules:
  0.0 197.5 jit_solution(16002461856078617909)
XLA Ops:
  0.6 189.1 %postnet_step.1 = (bf16[32,64,80]{2,1,0:T(8,128)(2,1)}, bf16[32,64,80]{2,1,0:T(8,128)(2,1)}, f32[5,2,16,80]{3,2,1,0:T(8,128)}, f32[3,5,2,16,512]{4,3,2,1,0:T(8,1...) custom-call(s32[64]{0:T(128)} %len_s.1, ...), custom_call_target="tpu_custom_call" | custom-call | tf_op jit(solution)/shard_map/postnet_step/pallas_call | solution.py:805
  189.8 0.0 copy-start.1
  189.8 0.0 copy-start
  189.8 2.0 %copy.29 = bf16[32,64,80]{2,1,0:T(8,128)(2,1)} copy(bf16[32,64,80]{2,1,0:T(8,128)(2,1)} %get-tuple-element.36) | data formatting | bytes 655360
  191.8 0.0 copy-done.1
  191.8 0.0 copy-start.3
  191.8 0.8 copy.30
  192.6 0.1 copy-done.3
  192.7 0.6 copy.31
  193.3 0.0 copy-done
  193.3 0.0 copy-start.2
  193.3 0.9 copy.32
  194.3 0.0 copy-done.2
  194.3 0.0 copy-start.5
  194.3 0.6 copy.33
  194.9 0.1 copy-done.5
  195.0 0.0 copy-start.4
  195.0 0.6 copy.34
  195.6 0.1 copy-done.4
  195.7 0.0 copy-start.7
  195.7 0.6 copy.35
  196.3 0.0 copy-done.7
  196.3 0.0 copy-start.6
  196.3 0.5 copy.36
  196.8 0.2 copy-done.6
  197.0 0.5 copy.37
Async XLA Ops:
  189.8 2.0 %copy-start.1 = (bf16[32,64,80]{2,1,0:T(8,128)(2,1)S(1)}, bf16[32,64,80]{2,1,0:T(8,128)(2,1)}, u32[]{:S(2)}) copy-start(bf16[32,64,80]{2,1,0:T(8,128)(2,1)} %get-tuple-element.37) | copy-start | bytes 983044
  189.8 3.6 %copy-start = (f32[3,5,2,16,512]{4,3,2,1,0:T(8,128)S(1)}, f32[3,5,2,16,512]{4,3,2,1,0:T(8,128)}, u32[]{:S(2)}) copy-start(f32[3,5,2,16,512]{4,3,2,1,0:T(8,128)} %get-tuple-element.21) | copy-start | bytes 2949124
  191.8 0.9 copy-start.3
  193.3 0.9 copy-start.2
  194.3 0.7 copy-start.5
  195.0 0.7 copy-start.4
  195.7 0.6 copy-start.7
  196.3 0.7 copy-start.6
